TPU v7x, 256 devices: a whole 4x4x8 slice. The times are simulated.
256 devices in a mesh: dp: 64 (over y, z, core), fsdp: 4 (over x).
Axes of the slice: x: 4, y: 4, z: 8, core: 2. Of those that a mesh axis runs over, the one named last changes fastest.
Arguments:
- tokens: bfloat16 [32768, 4096], P('dp', 'fsdp'), may hold values from -6 to 6
- query_weight: bfloat16 [4096, 2048], P('fsdp'), may hold values from -0.09375 to 0.09375
- neighbour_store: bfloat16 [512, 48, 32, 128], P('dp', None, 'fsdp'), may hold values from -170 to 170
- neighbours: int32 [512, 2], replicated, may hold values from 0 to 511, as said below
- attended_grad: bfloat16 [32768, 2048], P('dp', 'fsdp'), may hold values from -16 to 16
Outputs:
- attended: bfloat16 [32768, 2048], P('dp', 'fsdp')
- token_grad: bfloat16 [32768, 4096], P('dp', 'fsdp')
- weight_grad: float32 [4096, 2048], P('fsdp', 'dp')
- store_grad: float32 [512, 48, 32, 128], P('dp', None, 'fsdp')
Inputs may be any that keep to these rules, and one draw needn't show every extreme that they name: Entry e lies on store shard e // 8. Among the neighbours of the 8 spans of one index of dp, at most 1 lie on one shard, and some shard holds exactly 1.
All inputs are finite; a program needn't handle non-finite values.
Results may differ from a plain program's by a relative error of at most 0.028.
The roundings to bfloat16 on the way count: a program that leaves them out, or rounds other values in their place, can miss the bound.
Values may be sent and summed in bfloat16 or wider, within the bound.
A program may use at most 128 MiB of HBM per device.

v0:
```python
import math

import jax
import jax.numpy as jnp
from jax import lax
from jax.sharding import PartitionSpec as P

SPAN = 64


def soft_scores(query_blocks, key_rows, inverse_root):
    score_raw = (
        jnp.einsum("cqhd,ckhd->chqk", query_blocks, key_rows, preferred_element_type=jnp.float32)
        * inverse_root
    )
    row_peak = jnp.max(score_raw, axis=-1, keepdims=True)
    weights = jnp.exp(score_raw - row_peak)
    return weights / jnp.sum(weights, axis=-1, keepdims=True)


def on_device(tokens, query_weight, neighbour_store, neighbours, attended_grad):
    group_rows = tokens.shape[0]
    entries_here, near_len, heads_here, pair_width = neighbour_store.shape
    head_width = pair_width // 2
    slice_columns = heads_here * head_width
    span_count = group_rows // SPAN
    team_members = lax.axis_size("dp")
    my_group = lax.axis_index("dp")
    inverse_root = 1.0 / math.sqrt(head_width)
    asker_fields = lax.psum_scatter(
        lax.dot_general(
            query_weight, tokens, (((0,), (1,)), ((), ())), preferred_element_type=jnp.float32
        ),
        "fsdp",
        scatter_dimension=0,
        tiled=True,
    )
    queries = asker_fields.T.astype(jnp.bfloat16)
    query_blocks = queries.reshape(span_count, SPAN, heads_here, head_width)
    ref_table = neighbours.reshape(team_members, -1)
    ref_count = ref_table.shape[1]
    per_span = ref_count // span_count
    slot_cap = max(1, (ref_count + team_members - 1) // team_members)
    owner_table = ref_table // entries_here
    entry_table = ref_table % entries_here
    positions = jnp.arange(ref_count)
    earlier = positions[None, :] < positions[:, None]
    same_owner = owner_table[:, :, None] == owner_table[:, None, :]
    slot_table = jnp.sum(same_owner & earlier[None], axis=2)
    slot_ids = jnp.arange(slot_cap, dtype=jnp.int32)
    served = (owner_table == my_group)[:, :, None] & (
        slot_table[:, :, None] == slot_ids[None, None, :]
    )
    wanted = jnp.sum(jnp.where(served, entry_table[:, :, None] + 1, 0), axis=1).reshape(-1)
    pick_rows = jnp.maximum(wanted - 1, 0)
    outgoing = jnp.take(neighbour_store, pick_rows, axis=0)
    outgoing = jnp.where((wanted > 0)[:, None, None, None], outgoing, jnp.zeros_like(outgoing))
    arrived = lax.all_to_all(outgoing, "dp", split_axis=0, concat_axis=0, tiled=True)
    my_owners = lax.dynamic_index_in_dim(owner_table, my_group, 0, keepdims=False)
    my_slots = lax.dynamic_index_in_dim(slot_table, my_group, 0, keepdims=False)
    my_places = my_owners * slot_cap + my_slots
    brought_rows = jnp.take(arrived, my_places, axis=0)
    brought_rows = brought_rows.reshape(span_count, per_span * near_len, heads_here, pair_width)
    key_rows = brought_rows[..., :head_width]
    value_rows = brought_rows[..., head_width:]
    softmax_probs = soft_scores(query_blocks, key_rows, inverse_root)
    probs_low = softmax_probs.astype(jnp.bfloat16)
    attended = jnp.einsum(
        "chqk,ckhd->cqhd", probs_low, value_rows, preferred_element_type=jnp.float32
    )
    attended = attended.astype(jnp.bfloat16).reshape(group_rows, slice_columns)
    grad_blocks = attended_grad.reshape(span_count, SPAN, heads_here, head_width)
    prob_grad = jnp.einsum(
        "cqhd,ckhd->chqk", grad_blocks, value_rows, preferred_element_type=jnp.float32
    )
    row_terms = jnp.sum(softmax_probs * prob_grad, axis=-1, keepdims=True)
    score_grad = (softmax_probs * (prob_grad - row_terms)).astype(jnp.bfloat16)
    query_grad = (
        jnp.einsum("chqk,ckhd->cqhd", score_grad, key_rows, preferred_element_type=jnp.float32)
        * inverse_root
    )
    query_grad = query_grad.astype(jnp.bfloat16).reshape(group_rows, slice_columns)
    key_grad = (
        jnp.einsum("chqk,cqhd->ckhd", score_grad, query_blocks, preferred_element_type=jnp.float32)
        * inverse_root
    )
    value_grad = jnp.einsum(
        "chqk,cqhd->ckhd", probs_low, grad_blocks, preferred_element_type=jnp.float32
    )
    block_grad = jnp.concatenate([key_grad, value_grad], axis=-1).astype(jnp.bfloat16)
    block_grad = block_grad.reshape(ref_count, near_len, heads_here, pair_width)
    returning = jnp.zeros((team_members * slot_cap, near_len, heads_here, pair_width), jnp.bfloat16)
    returning = returning.at[my_places].set(block_grad)
    returned = lax.all_to_all(returning, "dp", split_axis=0, concat_axis=0, tiled=True)
    selector = (wanted[None, :] - 1 == jnp.arange(entries_here, dtype=jnp.int32)[:, None]).astype(
        jnp.bfloat16
    )
    store_grad = jnp.dot(
        selector, returned.reshape(team_members * slot_cap, -1), preferred_element_type=jnp.float32
    )
    store_grad = store_grad.reshape(entries_here, near_len, heads_here, pair_width)
    full_grad = lax.all_gather(query_grad, "fsdp", axis=1, tiled=True)
    token_grad = lax.dot_general(
        full_grad, query_weight, (((1,), (1,)), ((), ())), preferred_element_type=jnp.float32
    )
    token_grad = token_grad.astype(jnp.bfloat16)
    weight_share = lax.psum_scatter(
        lax.dot_general(
            full_grad, tokens, (((0,), (0,)), ((), ())), preferred_element_type=jnp.float32
        ),
        "dp",
        scatter_dimension=0,
        tiled=True,
    )
    weight_grad = weight_share.T
    return (attended, token_grad, weight_grad, store_grad)


def solution(mesh):
    return jax.shard_map(
        on_device,
        mesh=mesh,
        in_specs=(
            P("dp", "fsdp"),
            P("fsdp", None),
            P("dp", None, "fsdp", None),
            P(),
            P("dp", "fsdp"),
        ),
        out_specs=(P("dp", "fsdp"), P("dp", "fsdp"), P("fsdp", "dp"), P("dp", None, "fsdp", None)),
        check_vma=False,
    )
```

profile of v0, /device:TPU:1, one launch (start us, length us, event | category | flops | bytes accessed | tf_op | source)
XLA Modules:
  0.0 424.9 jit_solution(15507313983312609036)
XLA Ops:
  7.2 0.0 copy-start
  7.2 0.8 broadcast_compare_fusion.1
  8.0 0.8 copy.57
  8.9 0.2 copy.67
  9.1 0.1 reshape.188
  9.2 0.1 copy.58
  9.3 0.1 convert_reduce_fusion
  9.4 0.1 copy.69
  9.5 0.2 eq.52
  9.7 0.4 fusion.25
  10.1 0.1 reduce_sum.45
  10.2 0.1 reduce_sum.46
  10.3 4.0 gather_fusion
  14.3 6.2 %select_select_fusion = bf16[64,48,8,128]{3,2,1,0:T(8,128)(2,1)} fusion(bf16[64,48,8,128]{3,2,1,0:T(8,128)(2,1)} %gather_fusion, pred[64]{0:T(512)(128)(4,1)S(1)} %get-tuple-element.23, pred[64]{0:T(512)(128)(4,1)S(1)} %get-tuple-element.22), kind=kLoop, calls=%fused_computation.7 | loop fusion | flops 6291456 | bytes 12583040 | tf_op jit(solution)/shard_map/jit(_where)/select_n | solution.py:57
  20.6 13.3 %all-to-all-start = ((bf16[64,48,8,128]{3,2,1,0:T(8,128)(2,1)}), bf16[64,48,8,128]{3,2,1,0:T(8,128)(2,1)}, u32[]{:S(2)}, u32[]{:S(2)}) async-start(bf16[64,48,8,128]{3,2,1,0:T(8,128)(2,1)} %select_select_fusion), calls=%async_computation | async-start | bytes 12582912 | tf_op jit(solution)/shard_map/all_to_all | solution.py:58
  33.9 0.0 reduce-scatter.3.cloned.1.call-start
  34.0 6.5 %fusion.51 = f32[2048,512]{1,0:T(8,128)} fusion(bf16[1024,2048]{1,0:T(8,128)(2,1)} %param.6, bf16[512,1024]{1,0:T(8,128)(2,1)S(1)} %copy-done), kind=kOutput, calls=%fused_computation.78 | convolution fusion | flops 2147483648 | bytes 9437184 | tf_op jit(solution)/shard_map/dot_general | solution.py:31
  40.5 0.0 reduce-scatter.3.cloned.1.call-update
  40.5 0.2 all-gather.2.cloned.1.call-start
  40.8 0.2 add_reduce_fusion
  40.9 0.1 add.94
  41.0 0.1 broadcast_in_dim.48
  41.1 0.1 broadcast_in_dim.49
  41.2 0.3 copy-done.8
  41.5 0.5 reshape.191
  42.1 1.5 copy.77
  43.6 47.5 %reduce-scatter.3.cloned.1.call-done = f32[512,512]{1,0:T(8,128)} async-done(((f32[2048,512]{1,0:T(8,128)}), f32[512,512]{1,0:T(8,128)}) %reduce-scatter.3.cloned.1.call-update) | async-done | bytes 1048592 | tf_op jit(solution)/shard_map/reduce_scatter | solution.py:30
  91.0 1.3 convert_bitcast_fusion
  92.3 1.5 reshape.189
  93.9 80.9 %all-to-all-done = bf16[64,48,8,128]{3,2,1,0:T(8,128)(2,1)} async-done(((bf16[64,48,8,128]{3,2,1,0:T(8,128)(2,1)}), bf16[64,48,8,128]{3,2,1,0:T(8,128)(2,1)}, u32[]{:S(2)}, u32[]{:S(2)}) %all-to-all-start) | async-done | bytes 6291488 | tf_op jit(solution)/shard_map/all_to_all | solution.py:58
  174.7 4.7 %gather_fusion.1 = bf16[16,48,8,128]{3,2,1,0:T(8,128)(2,1)} fusion(bf16[64,48,8,128]{3,2,1,0:T(8,128)(2,1)} %all-to-all-done, s32[1024]{0:T(1024)S(1)} %pad_clamp_fusion), kind=kCustom, calls=%fused_computation.1 | custom fusion | bytes 3145792 | tf_op jit(solution)/shard_map/jit(_take)/gather | solution.py:62
  179.4 3.0 copy.70
  182.5 1.6 broadcast_select_fusion
  184.0 4.1 fusion.46
  188.1 3.6 fusion.3
  191.7 1.3 fusion.5
  193.0 0.3 copy-done.3
  193.3 0.7 fusion.9
  194.0 1.5 copy.74
  195.5 2.6 reshape.192
  198.1 0.0 all-gather.2.cloned.1.call-update
  198.1 3.3 fusion.8
  201.5 2.8 copy.78
  204.2 1.4 fusion.10
  205.6 2.7 copy.76
  208.4 2.7 pad_maximum_fusion
  211.1 4.1 broadcast.211
  215.2 4.9 %scatter_fusion = bf16[64,48,8,128]{3,2,1,0:T(8,128)(2,1)} fusion(bf16[64,48,8,128]{3,2,1,0:T(8,128)(2,1)} %broadcast.211, s32[16]{0:T(128)S(1)} %fusion.32, bf16[16,48,8,128]{3,2,1,0:T(8,128)(2,1)S(1)} %pad_maximum_fusion), kind=kCustom, calls=%fused_computation.2 | custom fusion | bytes 4718656 | tf_op jit(solution)/shard_map/scatter | solution.py:93
  220.1 6.1 %all-to-all-start.1 = ((bf16[64,48,8,128]{3,2,1,0:T(8,128)(2,1)}), bf16[64,48,8,128]{3,2,1,0:T(8,128)(2,1)}, u32[]{:S(2)}, u32[]{:S(2)}) async-start(bf16[64,48,8,128]{3,2,1,0:T(8,128)(2,1)} %scatter_fusion), calls=%async_computation.3 | async-start | bytes 12582912 | tf_op jit(solution)/shard_map/all_to_all | solution.py:94
  226.2 0.0 reduce-scatter.5.cloned.1.call-start
  226.3 1.9 all-gather.2.cloned.1.call-done
  228.1 7.2 %fusion.52 = f32[2048,1024]{1,0:T(8,128)} fusion(bf16[512,2048]{1,0:T(8,128)(2,1)} %all-gather.2.cloned.1.call-done, bf16[512,1024]{1,0:T(8,128)(2,1)S(1)} %copy-done), kind=kOutput, calls=%fused_computation.79 | convolution fusion | flops 2147483648 | bytes 11534336 | tf_op jit(solution)/shard_map/dot_general | solution.py:108
  235.3 0.0 reduce-scatter.5.cloned.1.call-update
  235.3 1.6 copy-done.4
  236.9 3.3 fusion.7
  240.2 1.7 copy.72
  241.9 1.4 reshape.190
  243.3 6.2 %convolution_convert_fusion.2 = bf16[512,1024]{1,0:T(8,128)(2,1)} fusion(bf16[512,2048]{1,0:T(8,128)(2,1)} %all-gather.2.cloned.1.call-done, bf16[1024,2048]{1,0:T(8,128)(2,1)} %param.6), kind=kOutput, calls=%fused_computation.22 | convolution fusion | flops 2148007936 | bytes 7340032 | tf_op jit(solution)/shard_map/dot_general | solution.py:103
  249.5 137.2 %all-to-all-done.1 = bf16[64,48,8,128]{3,2,1,0:T(8,128)(2,1)} async-done(((bf16[64,48,8,128]{3,2,1,0:T(8,128)(2,1)}), bf16[64,48,8,128]{3,2,1,0:T(8,128)(2,1)}, u32[]{:S(2)}, u32[]{:S(2)}) %all-to-all-start.1) | async-done | bytes 6291488 | tf_op jit(solution)/shard_map/all_to_all | solution.py:94
  386.7 6.8 %copy.105 = bf16[8,8,384,128]{3,1,2,0:T(8,128)(2,1)S(1)} copy(bf16[8,8,384,128]{3,2,1,0:T(8,128)(2,1)} %bitcast.20) | data formatting | bytes 12582912
  393.6 1.7 copy.89
  395.3 3.4 fusion.1
  398.7 1.4 copy.80
  400.2 18.2 %reduce-scatter.5.cloned.1.call-done = f32[32,1024]{1,0:T(8,128)} async-done(((f32[2048,1024]{1,0:T(8,128)}), f32[32,1024]{1,0:T(8,128)}) %reduce-scatter.5.cloned.1.call-update) | async-done | bytes 131088 | tf_op jit(solution)/shard_map/reduce_scatter | solution.py:107
  (23 shorter events, 0.1 us)
Async XLA Ops:
  7.2 26.8 %copy-start = (bf16[512,1024]{1,0:T(8,128)(2,1)S(1)}, bf16[512,1024]{1,0:T(8,128)(2,1)}, u32[]{:S(2)}) copy-start(bf16[512,1024]{1,0:T(8,128)(2,1)} %param.5) | copy-start | bytes 3145732
  7.2 3.1 copy-start.1
  20.6 154.2 %all-to-all-start = ((bf16[64,48,8,128]{3,2,1,0:T(8,128)(2,1)}), bf16[64,48,8,128]{3,2,1,0:T(8,128)(2,1)}, u32[]{:S(2)}, u32[]{:S(2)}) async-start(bf16[64,48,8,128]{3,2,1,0:T(8,128)(2,1)} %select_select_fusion), calls=%async_computation | async-start | bytes 12582912 | tf_op jit(solution)/shard_map/all_to_all | solution.py:58
  33.9 57.2 %reduce-scatter.3.cloned.1.call-start = ((), (), s32[]{:S(2)}) async-start(), calls=%async_computation.4 | async-start | bytes 5242880 | tf_op jit(solution)/shard_map/reduce_scatter | solution.py:30
  40.5 1.0 copy-start.8
  40.5 187.6 %all-gather.2.cloned.1.call-start = ((), (), s32[]{:S(2)}) async-start(), calls=%async_computation.5 | async-start | bytes 2621440 | tf_op jit(solution)/shard_map/all_gather | solution.py:102
  184.0 4.1 copy-start.2
  188.1 3.6 copy-start.6
  191.7 1.6 copy-start.3
  195.4 2.7 copy-start.7
  201.5 2.8 copy-start.5
  220.1 166.6 %all-to-all-start.1 = ((bf16[64,48,8,128]{3,2,1,0:T(8,128)(2,1)}), bf16[64,48,8,128]{3,2,1,0:T(8,128)(2,1)}, u32[]{:S(2)}, u32[]{:S(2)}) async-start(bf16[64,48,8,128]{3,2,1,0:T(8,128)(2,1)} %scatter_fusion), calls=%async_computation.3 | async-start | bytes 12582912 | tf_op jit(solution)/shard_map/all_to_all | solution.py:94
  226.2 192.1 %reduce-scatter.5.cloned.1.call-start = ((), (), s32[]{:S(2)}) async-start(), calls=%async_computation.6 | async-start | bytes 8519680 | tf_op jit(solution)/shard_map/reduce_scatter | solution.py:107
  235.3 1.6 copy-start.4
Sparse Core Ops, SparseCore 0:
  40.7 50.3 reduce-scatter.2
  198.2 29.8 all-gather.1
  235.4 182.8 reduce-scatter.4
where the time goes:
time: 430 us; the launch traced here: 425 us
  waiting for transfers between devices  286 us (67%)
  local copies, waits for them, and re-layouts  51 us (12%)
  matrix products  39.7 us (9%)
  starting transfers between devices  19.7 us (5%)
  other arithmetic  14.8 us (3%)
  between operations  14 us (3%)
    all_to_all x1, waiting for transfers between devices, on_device(): lax.all_to_all(returning, 'dp', split_axis=0, concat_axis=0, tiled=True)  137 us
    all_to_all x1, waiting for transfers between devices, on_device(): lax.all_to_all(outgoing, 'dp', split_axis=0, concat_axis=0, tiled=True)  80.9 us
    reduce_scatter x1, waiting for transfers between devices, on_device(): lax.psum_scatter(lax.dot_general(query_weight, tokens, (((0,), (1,)), (()...  47.5 us
    reduce_scatter x1, waiting for transfers between devices, on_device(): lax.psum_scatter(lax.dot_general(full_grad, tokens, (((0,), (0,)), ((), (...  18.2 us
    all_to_all x1, starting transfers between devices, on_device(): lax.all_to_all(outgoing, 'dp', split_axis=0, concat_axis=0, tiled=True)  13.3 us
    unnamed x22, local copies, waits for them, and re-layouts  13.1 us
  transfers between devices with their start and end apart: 5, of which 5 were waited for; matrix products, arithmetic and copies ran while one was open for 16% of the time, Pallas kernels for 0%

commit v1 on v0

v1 whole, which is shorter than its diff:
```python
import functools
import math

import jax
import jax.numpy as jnp
from jax import lax
from jax.experimental import pallas as pl
from jax.experimental.pallas import tpu as pltpu
from jax.sharding import PartitionSpec as P

SPAN = 64
NY, NZ = 4, 8
MESH = pl.DeviceIdType.MESH
Z_OFF = (0, -1, 1, -2, 2, -3, 3, 4)
J_OFF = ((0, 0), (0, 1), (-1, 0), (-1, 1), (1, 0), (1, 1), (2, 0), (2, 1))
VMEM_LIMIT = 56 * 1024 * 1024


def dp_of(y, z, c):
    return (y * NZ + z) * 2 + c


def exchange_kernel(by_target, code_ref, own, out, zp0, zp1, zp2, zm0, zm1, zm2, z4, sbuf, rl,
                    zs, zr, ysend, yrecv, rs, rr, fs, ls):
    me = lax.axis_index("dp")
    fs_id = lax.axis_index("fsdp")
    y, z, c = me // (2 * NZ), (me // 2) % NZ, me % 2
    half = own.shape[0] // 2

    def dev(dy, dz, dc):
        cc = c if dc == 0 else 1 - c
        return (dp_of((y + dy + NY) % NY, (z + dz + NZ) % NZ, cc), fs_id)

    greet = [dev(0, 1, 0), dev(0, -1, 0), dev(0, 0, 1),
             dev(1, 0, 0), dev(1, 0, 1), dev(-1, 0, 0), dev(-1, 0, 1)]
    barrier = pltpu.get_barrier_semaphore()
    for d in greet:
        pl.semaphore_signal(barrier, inc=1, device_id=d, device_id_type=MESH)
    pl.semaphore_wait(barrier, len(greet))

    def remote(src, dst, ssem, rsem, d):
        return pltpu.make_async_remote_copy(
            src_ref=src, dst_ref=dst, send_sem=ssem, recv_sem=rsem, device_id=d, device_id_type=MESH)

    up, down = dev(0, 1, 0), dev(0, -1, 0)
    zp, zm = [zp0, zp1, zp2], [zm0, zm1, zm2]
    ups = [remote(own, zp0, zs.at[0], zr.at[0], up),
           remote(zp0, zp1, zs.at[1], zr.at[1], up),
           remote(zp1, zp2, zs.at[2], zr.at[2], up),
           remote(zp2.at[pl.ds(0, half)], z4.at[pl.ds(0, half)], zs.at[3], zr.at[3], up)]
    downs = [remote(own, zm0, zs.at[4], zr.at[4], down),
             remote(zm0, zm1, zs.at[5], zr.at[5], down),
             remote(zm1, zm2, zs.at[6], zr.at[6], down),
             remote(zm2.at[pl.ds(half, half)], z4.at[pl.ds(half, half)], zs.at[7], zr.at[7], down)]
    sets = [own, zp0, zm0, zp1, zm1, zp2, zm2, z4]
    locals_, sends, relays, forwards = [], [], [], []

    def process(k):
        origin = dp_of(y, (z + Z_OFF[k] + NZ) % NZ, c)
        for i, (dy, dc) in enumerate(J_OFF):
            target = dev(dy, 0, dc)[0]
            place = origin * 64 + target if by_target else target * 64 + origin
            code = code_ref[place]
            pick = (code // 8) % 16 if by_target else code % 8
            sbuf[k, i] = sets[k][pick]
        cp = pltpu.make_async_copy(sbuf.at[k, 0], out.at[k], ls.at[k])
        cp.start()
        locals_.append(cp)
        for i, j in ((1, 1), (4, 2), (5, 3), (2, 4), (3, 5)):
            dy, dc = J_OFF[i]
            cp = remote(sbuf.at[k, i], out.at[j * 8 + k], ysend.at[k, i], yrecv.at[j * 8 + k], dev(dy, 0, dc))
            cp.start()
            sends.append(cp)
        cp = remote(sbuf.at[k, pl.ds(6, 2)], rl.at[k], rs.at[k], rr.at[k], dev(1 if k % 2 == 0 else -1, 0, 0))
        cp.start()
        relays.append(cp)

    def relay(k):
        relays[k].wait_recv()
        for dc in range(2):
            cp = remote(rl.at[k, dc], out.at[(6 + dc) * 8 + k], fs.at[k, dc], yrecv.at[(6 + dc) * 8 + k],
                        dev(1 if k % 2 == 0 else -1, 0, dc))
            cp.start()
            forwards.append(cp)

    ups[0].start()
    downs[0].start()
    process(0)
    for s in range(3):
        ups[s].wait_recv()
        ups[s + 1].start()
        downs[s].wait_recv()
        downs[s + 1].start()
        process(1 + 2 * s)
        process(2 + 2 * s)
        if s == 1:
            relay(0)
        if s == 2:
            relay(1)
            relay(2)
    ups[3].wait_recv()
    downs[3].wait_recv()
    process(7)
    for k in range(3, 8):
        relay(k)
    for cp in locals_:
        cp.wait()
    for cp in sends:
        cp.wait()
    for cp in forwards:
        cp.wait()
    for cp in relays + ups + downs:
        cp.wait_send()


def exchange(code, own, by_target, collective_id):
    n, rows, cols = own.shape
    blocks = pltpu.VMEM((n, rows, cols), own.dtype)
    dma = pltpu.SemaphoreType.DMA
    moved = 64 * rows * cols * 2
    return pl.pallas_call(
        functools.partial(exchange_kernel, by_target),
        out_shape=jax.ShapeDtypeStruct((64, rows, cols), own.dtype),
        in_specs=[pl.BlockSpec(memory_space=pltpu.SMEM), pl.BlockSpec(memory_space=pltpu.VMEM)],
        out_specs=pl.BlockSpec(memory_space=pl.ANY),
        scratch_shapes=[blocks] * 7 + [
            pltpu.VMEM((8, 8, rows, cols), own.dtype),
            pltpu.VMEM((8, 2, rows, cols), own.dtype),
            dma((8,)), dma((8,)), dma((8, 8)), dma((64,)), dma((8,)), dma((8,)), dma((8, 2)), dma((8,)),
        ],
        compiler_params=pltpu.CompilerParams(
            collective_id=collective_id, has_side_effects=True, vmem_limit_bytes=VMEM_LIMIT),
        cost_estimate=pl.CostEstimate(flops=0, bytes_accessed=40 * moved, transcendentals=0),
        name="exchange_back" if by_target else "exchange_out",
    )(code, own)


def attention_kernel(pos_ref, q_ref, g_ref, kv0_ref, kv1_ref, att_ref, qg_ref, bg_ref):
    heads = kv0_ref.shape[1]
    width = q_ref.shape[1] // heads
    near = kv0_ref.shape[2]
    root = 1.0 / math.sqrt(width)
    zero = jnp.zeros((SPAN, width), jnp.bfloat16)
    nt = (((1,), (1,)), ((), ()))
    nn = (((1,), (0,)), ((), ()))
    tn = (((0,), (0,)), ((), ()))

    def dot(a, b, dims):
        return lax.dot_general(a, b, dims, preferred_element_type=jnp.float32)

    for h in range(heads):
        cols = slice(h * width, (h + 1) * width)
        q, g = q_ref[:, cols], g_ref[:, cols]
        kv = jnp.concatenate([kv0_ref[0, h], kv1_ref[0, h]], axis=0)
        both = jnp.concatenate(
            [jnp.concatenate([q, zero], axis=1), jnp.concatenate([zero, g], axis=1)], axis=0)
        raw = dot(both, kv, nt)
        score = raw[:SPAN] * root
        prob_grad = raw[SPAN:]
        weights = jnp.exp(score - jnp.max(score, axis=-1, keepdims=True))
        probs = weights / jnp.sum(weights, axis=-1, keepdims=True)
        low = probs.astype(jnp.bfloat16)
        term = jnp.sum(probs * prob_grad, axis=-1, keepdims=True)
        sg = (probs * (prob_grad - term)).astype(jnp.bfloat16)
        applied = dot(jnp.concatenate([low, sg], axis=0), kv, nn)
        att_ref[:, cols] = applied[:SPAN, width:].astype(jnp.bfloat16)
        qg_ref[:, cols] = (applied[SPAN:, :width] * root).astype(jnp.bfloat16)
        back = dot(jnp.concatenate([sg, low], axis=0), both, tn)
        lane = lax.broadcasted_iota(jnp.int32, back.shape, 1)
        back = (back * jnp.where(lane < width, root, 1.0)).astype(jnp.bfloat16)
        bg_ref[0, h] = back[:near]
        bg_ref[1, h] = back[near:]


def attention(pos, queries, grads, blocks):
    rows, cols = queries.shape
    spans = rows // SPAN
    _, heads, near, pair = blocks.shape
    kv = lambda n: pl.BlockSpec((1, heads, near, pair), lambda i, pos: (pos[2 * i + n], 0, 0, 0))
    flat = pl.BlockSpec((SPAN, cols), lambda i, pos: (i, 0))
    return pl.pallas_call(
        attention_kernel,
        grid_spec=pltpu.PrefetchScalarGridSpec(
            num_scalar_prefetch=1,
            grid=(spans,),
            in_specs=[flat, flat, kv(0), kv(1)],
            out_specs=[flat, flat, pl.BlockSpec((2, heads, near, pair), lambda i, pos: (i, 0, 0, 0))],
        ),
        out_shape=[
            jax.ShapeDtypeStruct((rows, cols), jnp.bfloat16),
            jax.ShapeDtypeStruct((rows, cols), jnp.bfloat16),
            jax.ShapeDtypeStruct((2 * spans, heads, near, pair), jnp.bfloat16),
        ],
        compiler_params=pltpu.CompilerParams(vmem_limit_bytes=VMEM_LIMIT),
        name="attention",
    )(pos, queries, grads, blocks, blocks)


def gather_sum_kernel(code_ref, blk_ref, out_ref, acc):
    h = pl.program_id(0)
    acc[...] = jnp.zeros_like(acc)

    def body(i, carry):
        code = code_ref[i]

        @pl.when(code >= 128)
        def _():
            e = code % 8
            acc[e] += blk_ref[i, 0].astype(jnp.float32)

        return carry

    lax.fori_loop(0, 64, body, 0)
    out_ref[0] = acc[...]


def gather_sum(codes, blocks):
    _, heads, near, pair = blocks.shape
    return pl.pallas_call(
        gather_sum_kernel,
        grid=(heads,),
        in_specs=[
            pl.BlockSpec(memory_space=pltpu.SMEM),
            pl.BlockSpec((64, 1, near, pair), lambda h: (0, h, 0, 0)),
        ],
        out_specs=pl.BlockSpec((1, 8, near, pair), lambda h: (h, 0, 0, 0)),
        out_shape=jax.ShapeDtypeStruct((heads, 8, near, pair), jnp.float32),
        scratch_shapes=[pltpu.VMEM((8, near, pair), jnp.float32)],
        compiler_params=pltpu.CompilerParams(vmem_limit_bytes=VMEM_LIMIT),
        name="gather_sum",
    )(codes, blocks)


def slot_devices(me):
    y, z, c = me // (2 * NZ), (me // 2) % NZ, me % 2
    ys = jnp.array([j[0] for j in J_OFF], jnp.int32)[:, None]
    cs = jnp.array([j[1] for j in J_OFF], jnp.int32)[:, None]
    zs = jnp.array(Z_OFF, jnp.int32)[None, :]
    return dp_of((y + ys + NY) % NY, (z + zs + NZ) % NZ, (c + cs) % 2).reshape(-1)


def on_device(tokens, query_weight, neighbour_store, neighbours, attended_grad):
    entries_here, near, heads, pair = neighbour_store.shape
    me = lax.axis_index("dp")
    fields = lax.psum_scatter(
        lax.dot_general(
            query_weight, tokens, (((0,), (1,)), ((), ())), preferred_element_type=jnp.float32
        ),
        "fsdp",
        scatter_dimension=0,
        tiled=True,
    )
    queries = fields.T.astype(jnp.bfloat16)

    refs = neighbours.reshape(64, -1)
    order = jnp.arange(refs.shape[1], dtype=jnp.int32)[None, :]
    word = 128 + 8 * order + refs % entries_here
    shard = jnp.arange(64, dtype=jnp.int32)
    table = jnp.max(
        jnp.where((refs // entries_here)[:, :, None] == shard, word[:, :, None], 0), axis=1)
    code = table.reshape(-1)

    slots = slot_devices(me)
    mine = lax.dynamic_index_in_dim(refs, me, 0, keepdims=False) // entries_here
    pos = jnp.sum(
        jnp.where(mine[:, None] == slots[None, :], jnp.arange(64, dtype=jnp.int32)[None, :], 0), axis=1)

    store = neighbour_store.transpose(0, 2, 1, 3).reshape(entries_here, heads * near, pair)
    got = exchange(code, store, False, 0).reshape(64, heads, near, pair)
    attended, query_grad, block_grad = attention(pos, queries, attended_grad, got)

    full_grad = lax.all_gather(query_grad, "fsdp", axis=1, tiled=True)
    token_grad = lax.dot_general(
        full_grad, query_weight, (((1,), (1,)), ((), ())), preferred_element_type=jnp.float32
    ).astype(jnp.bfloat16)
    weight_share = lax.psum_scatter(
        lax.dot_general(
            full_grad, tokens, (((0,), (0,)), ((), ())), preferred_element_type=jnp.float32
        ),
        "dp",
        scatter_dimension=0,
        tiled=True,
    )
    weight_grad = weight_share.T

    back = exchange(code, block_grad.reshape(-1, heads * near, pair), True, 1)
    column = jnp.take(table, slots, axis=0)
    column = lax.dynamic_index_in_dim(column, me, 1, keepdims=False)
    summed = gather_sum(column, back.reshape(64, heads, near, pair))
    store_grad = summed.transpose(1, 2, 0, 3)
    return (attended, token_grad, weight_grad, store_grad)


def solution(mesh):
    return jax.shard_map(
        on_device,
        mesh=mesh,
        in_specs=(
            P("dp", "fsdp"),
            P("fsdp", None),
            P("dp", None, "fsdp", None),
            P(),
            P("dp", "fsdp"),
        ),
        out_specs=(P("dp", "fsdp"), P("dp", "fsdp"), P("fsdp", "dp"), P("dp", None, "fsdp", None)),
        check_vma=False,
    )
```

time: 430 us -> 388 us (0.902)
  Pallas kernels: 0 us -> 311 us
  waiting for transfers between devices: 286 us -> 30.8 us
  local copies, waits for them, and re-layouts: 51 us -> 7.91 us
  matrix products: 39.7 us -> 17.1 us
  starting transfers between devices: 19.7 us -> 0.3 us
  other arithmetic: 14.8 us -> 4.02 us
    pallas_call x0 -> x4, Pallas kernels: none -> 311 us  [the longest x2 279 us: exchange(): pl.pallas_call(functools.partial(exchange_kernel, by_target), out_shape=j...]
    all_to_all x2 -> x0, waiting for transfers between devices: 218 us -> none  [the longest x1 137 us: on_device(): lax.all_to_all(returning, 'dp', split_axis=0, concat_axis=0, tiled=True)]
    reduce_scatter x1, waiting for transfers between devices: 47.5 us -> 0.01 us  [on_device(): lax.psum_scatter(lax.dot_general(query_weight, tokens, (((0,), (1,)), (()...]
    all_gather x1, waiting for transfers between devices: 1.86 us -> 30.7 us  [on_device(): full_grad = lax.all_gather(query_grad, 'fsdp', axis=1, tiled=True)]
    all_to_all x2 -> x0, starting transfers between devices: 19.4 us -> none  [the longest x1 13.3 us: on_device(): lax.all_to_all(outgoing, 'dp', split_axis=0, concat_axis=0, tiled=True)]
    reduce_scatter x1, waiting for transfers between devices: 18.2 us -> 0.01 us  [on_device(): lax.psum_scatter(lax.dot_general(full_grad, tokens, (((0,), (0,)), ((), (...]
    dot_general x6 -> x0, matrix products: 15.8 us -> none  [the longest x1 3.59 us: on_device(): jnp.einsum('cqhd,ckhd->chqk', grad_blocks, value_rows, preferred_element_...]
    gather x3 -> x1, local copies, waits for them, and re-layouts: 11.7 us -> 0.6 us  [on_device(): column = jnp.take(table, slots, axis=0)]
  transfers between devices with their start and end apart: 5 -> 3, of which waited for: 5 -> 1; matrix products, arithmetic and copies ran while one was open for 16% -> 3% of each run, Pallas kernels for 0% -> 75%
where the time goes in v1:
time: 388 us; the launch traced here: 385 us
  Pallas kernels  311 us (80%)
  waiting for transfers between devices  30.8 us (8%)
  matrix products  17.1 us (4%)
  between operations  13.9 us (4%)
  local copies, waits for them, and re-layouts  7.91 us (2%)
  other arithmetic  4.02 us (1%)
    pallas_call x2, Pallas kernels, exchange(): pl.pallas_call(functools.partial(exchange_kernel, by_target), out_shape=j...  279 us
    all_gather x1, waiting for transfers between devices, on_device(): full_grad = lax.all_gather(query_grad, 'fsdp', axis=1, tiled=True)  30.7 us
    pallas_call x1, Pallas kernels, attention(): pl.pallas_call(attention_kernel, grid_spec=pltpu.PrefetchScalarGridSpec(n...  21.7 us
    pallas_call x1, Pallas kernels, gather_sum(): pl.pallas_call(gather_sum_kernel, grid=(heads,), in_specs=[pl.BlockSpec(m...  10.8 us
  transfers between devices with their start and end apart: 3, of which 1 were waited for; matrix products, arithmetic and copies ran while one was open for 3% of the time, Pallas kernels for 75%

profile of v1, /device:TPU:1, one launch (start us, length us, event | category | flops | bytes accessed | tf_op | source)
XLA Modules:
  0.0 385.3 jit_solution(6120152430540418279)
XLA Ops:
  7.2 0.0 copy-start
  7.2 0.0 reduce-scatter.3.cloned.1.call-start
  7.2 1.2 copy-done
  8.4 6.5 %fusion.10 = f32[2048,512]{0,1:T(8,128)} fusion(bf16[512,1024]{1,0:T(8,128)(2,1)S(1)} %copy-done, bf16[1024,2048]{1,0:T(8,128)(2,1)} %param.9), kind=kOutput, calls=%fused_computation.43 | convolution fusion | flops 2147483648 | bytes 9437184 | tf_op jit(solution)/shard_map/dot_general | solution.py:246
  14.9 0.0 copy-start.7
  14.9 0.0 copy-start.3
  14.9 0.0 copy-start.4
  14.9 0.0 copy-start.2
  15.0 0.0 copy-start.1
  15.0 0.0 reduce-scatter.3.cloned.1.call-update
  15.0 0.0 all-gather.2.cloned.1.call-start
  15.1 0.5 copy-done.7
  15.6 0.0 copy-done.3
  15.6 0.0 copy-done.4
  15.6 0.1 multiply_add_fusion
  15.7 0.1 add.204
  15.8 0.0 copy-done.2
  15.8 0.1 copy.19
  16.0 0.1 reshape.232
  16.1 0.4 select_reduce_fusion
  16.5 0.7 reshape.233.code_ref
  17.2 0.0 copy-done.1
  17.2 1.0 copy.21
  18.2 104.8 %exchange_out.1 = bf16[64,384,128]{2,1,0:T(8,128)(2,1)} custom-call(s32[4096]{0:T(1024)} %reshape.233.code_ref, bf16[8,384,128]{2,1,0:T(8,128)(2,1)} %bitcast.29), custom_call_target="tpu_custom_call" | custom-call | bytes 251658240 | tf_op jit(solution)/shard_map/exchange_out/pallas_call | solution.py:121
  123.1 0.7 select_reduce_fusion.1.pos_ref
  123.8 0.0 reduce-scatter.3.cloned.1.call-done
  123.8 2.1 convert_bitcast_fusion.q_ref
  125.8 21.7 %attention.1 = (bf16[512,512]{1,0:T(8,128)(2,1)}, bf16[512,512]{1,0:T(8,128)(2,1)}, bf16[16,8,48,128]{3,2,1,0:T(8,128)(2,1)}) custom-call(s32[16]{0:T(128)} %select_reduce_fusion.1.pos_ref, bf16[512,512]{1,0:T(8,128)(2,1)} %convert_bitcast_fusion.q_ref, bf16[512,512]{1,0:T(8,128)(2,1)} %g_ref.1, bf16[64,8,48,128]{3,2,1,0:T(8,128)(2,1)} %bitcast.25, ...), custom_call_target="tpu_custom_call" | custom-call | tf_op jit(solution)/shard_map/attention/pallas_call | solution.py:181
  147.5 0.0 all-gather.2.cloned.1.call-update
  147.5 0.2 reduce-scatter.5.cloned.1.call-start
  147.8 30.7 %all-gather.2.cloned.1.call-done = bf16[512,2048]{1,0:T(8,128)(2,1)} async-done(((bf16[512,512]{1,0:T(8,128)(2,1)}), bf16[512,2048]{1,0:T(8,128)(2,1)}) %all-gather.2.cloned.1.call-update) | async-done | bytes 2097168 | tf_op jit(solution)/shard_map/all_gather | solution.py:272
  178.5 7.2 %fusion.9 = f32[2048,1024]{1,0:T(8,128)} fusion(bf16[512,2048]{1,0:T(8,128)(2,1)} %all-gather.2.cloned.1.call-done, bf16[512,1024]{1,0:T(8,128)(2,1)S(1)} %copy-done), kind=kOutput, calls=%fused_computation.42 | convolution fusion | flops 2147483648 | bytes 11534336 | tf_op jit(solution)/shard_map/dot_general | solution.py:277
  185.7 0.0 reduce-scatter.5.cloned.1.call-update
  185.7 0.1 add.211
  185.8 0.6 gather_fusion
  186.4 0.7 fusion.1.code_ref
  187.1 174.0 %exchange_back.1 = bf16[64,384,128]{2,1,0:T(8,128)(2,1)} custom-call(s32[4096]{0:T(1024)} %reshape.233.code_ref, bf16[16,384,128]{2,1,0:T(8,128)(2,1)} %bitcast.30), custom_call_target="tpu_custom_call" | custom-call | bytes 251658240 | tf_op jit(solution)/shard_map/exchange_back/pallas_call | solution.py:121
  361.1 0.0 copy-start.5
  361.1 0.0 copy-start.6
  361.1 10.8 %gather_sum.1 = f32[8,8,48,128]{3,2,1,0:T(8,128)} custom-call(s32[64]{0:T(128)} %fusion.1.code_ref, bf16[64,8,48,128]{3,2,1,0:T(8,128)(2,1)} %bitcast.27), custom_call_target="tpu_custom_call" | custom-call | tf_op jit(solution)/shard_map/gather_sum/pallas_call | solution.py:219
  372.0 3.5 copy.22
  375.5 0.0 copy-done.5
  375.5 0.0 copy-done.6
  375.5 3.3 convolution_convert_fusion
  378.8 0.0 reduce-scatter.5.cloned.1.call-done
  (8 shorter events, 0.1 us)
Async XLA Ops:
  7.2 1.2 copy-start
  7.2 116.6 %reduce-scatter.3.cloned.1.call-start = ((), (), s32[]{:S(2)}) async-start(), calls=%async_computation.2 | async-start | bytes 5242880 | tf_op jit(solution)/shard_map/reduce_scatter | solution.py:245
  14.9 0.7 copy-start.7
  14.9 0.7 copy-start.3
  14.9 0.7 copy-start.4
  14.9 0.9 copy-start.2
  15.0 2.2 copy-start.1
  15.0 163.5 %all-gather.2.cloned.1.call-start = ((), (), s32[]{:S(2)}) async-start(), calls=%async_computation.3 | async-start | bytes 2621440 | tf_op jit(solution)/shard_map/all_gather | solution.py:272
  147.5 231.3 %reduce-scatter.5.cloned.1.call-start = ((), (), s32[]{:S(2)}) async-start(), calls=%async_computation.4 | async-start | bytes 8519680 | tf_op jit(solution)/shard_map/reduce_scatter | solution.py:276
  361.1 14.3 %copy-start.5 = (bf16[1024,2048]{1,0:T(8,128)(2,1)S(1)}, bf16[1024,2048]{1,0:T(8,128)(2,1)}, u32[]{:S(2)}) copy-start(bf16[1024,2048]{1,0:T(8,128)(2,1)} %param.9) | copy-start | bytes 12582916
  361.1 14.3 %copy-start.6 = (bf16[512,2048]{1,0:T(8,128)(2,1)S(1)}, bf16[512,2048]{1,0:T(8,128)(2,1)}, u32[]{:S(2)}) copy-start(bf16[512,2048]{1,0:T(8,128)(2,1)} %all-gather.2.cloned.1.call-done) | copy-start | bytes 6291460
Sparse Core Ops, SparseCore 0:
  15.1 53.1 reduce-scatter.2
  147.7 30.8 all-gather.1
  185.9 162.1 reduce-scatter.4

commit v2 on v1

--- a/solution.py
+++ b/solution.py
@@ -13,126 +13,365 @@
 MESH = pl.DeviceIdType.MESH
 Z_OFF = (0, -1, 1, -2, 2, -3, 3, 4)
 J_OFF = ((0, 0), (0, 1), (-1, 0), (-1, 1), (1, 0), (1, 1), (2, 0), (2, 1))
-VMEM_LIMIT = 56 * 1024 * 1024
+VMEM_LIMIT = 60 * 1024 * 1024
 
 
 def dp_of(y, z, c):
     return (y * NZ + z) * 2 + c
 
 
-def exchange_kernel(by_target, code_ref, own, out, zp0, zp1, zp2, zm0, zm1, zm2, z4, sbuf, rl,
-                    zs, zr, ysend, yrecv, rs, rr, fs, ls):
-    me = lax.axis_index("dp")
-    fs_id = lax.axis_index("fsdp")
-    y, z, c = me // (2 * NZ), (me // 2) % NZ, me % 2
+class Place:
+    def __init__(self):
+        me = lax.axis_index("dp")
+        self.x = lax.axis_index("fsdp")
+        self.y, self.z, self.c = me // (2 * NZ), (me // 2) % NZ, me % 2
+
+    def dp(self, dy, dz, dc):
+        return dp_of((self.y + dy + NY) % NY, (self.z + dz + NZ) % NZ, (self.c + dc) % 2)
+
+    def dev(self, dy=0, dz=0, dc=0, dx=0):
+        return (self.dp(dy, dz, dc), (self.x + dx + 4) % 4)
+
+
+def greet(devices):
+    barrier = pltpu.get_barrier_semaphore()
+    for d in devices:
+        pl.semaphore_signal(barrier, inc=1, device_id=d, device_id_type=MESH)
+    pl.semaphore_wait(barrier, len(devices))
+
+
+def remote(src, dst, ssem, rsem, d):
+    return pltpu.make_async_remote_copy(
+        src_ref=src, dst_ref=dst, send_sem=ssem, recv_sem=rsem, device_id=d, device_id_type=MESH)
+
+
+def plane_partners(p):
+    return [p.dev(dy, 0, dc) for dy, dc in J_OFF[1:]]
+
+
+def plane_send(p, out, k, hh, blocks, ysend, yrecv, ls):
+    local = pltpu.make_async_copy(blocks(0), out.at[k, hh], ls.at[k, hh])
+    local.start()
+    sends = []
+    for i, j in ((1, 1), (6, 6), (7, 7), (4, 2), (5, 3), (2, 4), (3, 5)):
+        dy, dc = J_OFF[i]
+        cp = remote(blocks(i), out.at[j * 8 + k, hh], ysend.at[k, hh, i], yrecv.at[j * 8 + k, hh],
+                    p.dev(dy, 0, dc))
+        cp.start()
+        sends.append(cp)
+    return local, sends
+
+
+def out_kernel(code_ref, own, out, zp0, zp1, zp2, zm0, zm1, zm2, z4, sbuf,
+               zs, zr, ysend, yrecv, ls):
+    p = Place()
     half = own.shape[0] // 2
-
-    def dev(dy, dz, dc):
-        cc = c if dc == 0 else 1 - c
-        return (dp_of((y + dy + NY) % NY, (z + dz + NZ) % NZ, cc), fs_id)
-
-    greet = [dev(0, 1, 0), dev(0, -1, 0), dev(0, 0, 1),
-             dev(1, 0, 0), dev(1, 0, 1), dev(-1, 0, 0), dev(-1, 0, 1)]
-    barrier = pltpu.get_barrier_semaphore()
-    for d in greet:
-        pl.semaphore_signal(barrier, inc=1, device_id=d, device_id_type=MESH)
-    pl.semaphore_wait(barrier, len(greet))
-
-    def remote(src, dst, ssem, rsem, d):
-        return pltpu.make_async_remote_copy(
-            src_ref=src, dst_ref=dst, send_sem=ssem, recv_sem=rsem, device_id=d, device_id_type=MESH)
-
-    up, down = dev(0, 1, 0), dev(0, -1, 0)
+    up, down = p.dev(0, 1), p.dev(0, -1)
+    greet([up, down] + plane_partners(p))
     zp, zm = [zp0, zp1, zp2], [zm0, zm1, zm2]
-    ups = [remote(own, zp0, zs.at[0], zr.at[0], up),
-           remote(zp0, zp1, zs.at[1], zr.at[1], up),
-           remote(zp1, zp2, zs.at[2], zr.at[2], up),
-           remote(zp2.at[pl.ds(0, half)], z4.at[pl.ds(0, half)], zs.at[3], zr.at[3], up)]
-    downs = [remote(own, zm0, zs.at[4], zr.at[4], down),
-             remote(zm0, zm1, zs.at[5], zr.at[5], down),
-             remote(zm1, zm2, zs.at[6], zr.at[6], down),
-             remote(zm2.at[pl.ds(half, half)], z4.at[pl.ds(half, half)], zs.at[7], zr.at[7], down)]
-    sets = [own, zp0, zm0, zp1, zm1, zp2, zm2, z4]
-    locals_, sends, relays, forwards = [], [], [], []
-
-    def process(k):
-        origin = dp_of(y, (z + Z_OFF[k] + NZ) % NZ, c)
+    lo, hi = pl.ds(0, half), pl.ds(half, half)
+    ups, downs = [], []
+    for hh in range(2):
+        ups.append([remote(own.at[:, hh], zp0[hh], zs.at[0, hh], zr.at[0, hh], up),
+                    remote(zp0[hh], zp1[hh], zs.at[1, hh], zr.at[1, hh], up),
+                    remote(zp1[hh], zp2[hh], zs.at[2, hh], zr.at[2, hh], up),
+                    remote(zp2[hh].at[lo], z4[hh].at[lo], zs.at[3, hh], zr.at[3, hh], up)])
+        downs.append([remote(own.at[:, hh], zm0[hh], zs.at[4, hh], zr.at[4, hh], down),
+                      remote(zm0[hh], zm1[hh], zs.at[5, hh], zr.at[5, hh], down),
+                      remote(zm1[hh], zm2[hh], zs.at[6, hh], zr.at[6, hh], down),
+                      remote(zm2[hh].at[hi], z4[hh].at[hi], zs.at[7, hh], zr.at[7, hh], down)])
+    sets = [None, zp0, zm0, zp1, zm1, zp2, zm2, z4]
+    started = []
+
+    def process(k, hh):
+        origin = p.dp(0, Z_OFF[k], 0)
         for i, (dy, dc) in enumerate(J_OFF):
-            target = dev(dy, 0, dc)[0]
-            place = origin * 64 + target if by_target else target * 64 + origin
-            code = code_ref[place]
-            pick = (code // 8) % 16 if by_target else code % 8
-            sbuf[k, i] = sets[k][pick]
-        cp = pltpu.make_async_copy(sbuf.at[k, 0], out.at[k], ls.at[k])
-        cp.start()
-        locals_.append(cp)
-        for i, j in ((1, 1), (4, 2), (5, 3), (2, 4), (3, 5)):
-            dy, dc = J_OFF[i]
-            cp = remote(sbuf.at[k, i], out.at[j * 8 + k], ysend.at[k, i], yrecv.at[j * 8 + k], dev(dy, 0, dc))
-            cp.start()
-            sends.append(cp)
-        cp = remote(sbuf.at[k, pl.ds(6, 2)], rl.at[k], rs.at[k], rr.at[k], dev(1 if k % 2 == 0 else -1, 0, 0))
-        cp.start()
-        relays.append(cp)
-
-    def relay(k):
-        relays[k].wait_recv()
-        for dc in range(2):
-            cp = remote(rl.at[k, dc], out.at[(6 + dc) * 8 + k], fs.at[k, dc], yrecv.at[(6 + dc) * 8 + k],
-                        dev(1 if k % 2 == 0 else -1, 0, dc))
-            cp.start()
-            forwards.append(cp)
-
-    ups[0].start()
-    downs[0].start()
-    process(0)
+            pick = code_ref[p.dp(dy, 0, dc) * 64 + origin] % 8
+            sbuf[k, hh, i] = own[pick, hh] if k == 0 else sets[k][hh][pick]
+        started.append(plane_send(p, out, k, hh, lambda i: sbuf.at[k, hh, i], ysend, yrecv, ls))
+
+    for hh in range(2):
+        ups[hh][0].start()
+        downs[hh][0].start()
+    for hh in range(2):
+        process(0, hh)
     for s in range(3):
-        ups[s].wait_recv()
-        ups[s + 1].start()
-        downs[s].wait_recv()
-        downs[s + 1].start()
-        process(1 + 2 * s)
-        process(2 + 2 * s)
-        if s == 1:
-            relay(0)
-        if s == 2:
-            relay(1)
-            relay(2)
-    ups[3].wait_recv()
-    downs[3].wait_recv()
-    process(7)
-    for k in range(3, 8):
-        relay(k)
-    for cp in locals_:
-        cp.wait()
-    for cp in sends:
-        cp.wait()
-    for cp in forwards:
-        cp.wait()
-    for cp in relays + ups + downs:
-        cp.wait_send()
-
-
-def exchange(code, own, by_target, collective_id):
-    n, rows, cols = own.shape
+        for hh in range(2):
+            ups[hh][s].wait_recv()
+            ups[hh][s + 1].start()
+            downs[hh][s].wait_recv()
+            downs[hh][s + 1].start()
+            process(1 + 2 * s, hh)
+            process(2 + 2 * s, hh)
+    for hh in range(2):
+        ups[hh][3].wait_recv()
+        downs[hh][3].wait_recv()
+        process(7, hh)
+    for local, sends in started:
+        local.wait()
+        for cp in sends:
+            cp.wait()
+    for hh in range(2):
+        for cp in ups[hh] + downs[hh]:
+            cp.wait_send()
+
+
+def exchange_out(code, own):
+    n, _, rows, cols = own.shape
     blocks = pltpu.VMEM((n, rows, cols), own.dtype)
     dma = pltpu.SemaphoreType.DMA
-    moved = 64 * rows * cols * 2
     return pl.pallas_call(
-        functools.partial(exchange_kernel, by_target),
-        out_shape=jax.ShapeDtypeStruct((64, rows, cols), own.dtype),
+        out_kernel,
+        out_shape=jax.ShapeDtypeStruct((64, 2, rows, cols), own.dtype),
         in_specs=[pl.BlockSpec(memory_space=pltpu.SMEM), pl.BlockSpec(memory_space=pltpu.VMEM)],
         out_specs=pl.BlockSpec(memory_space=pl.ANY),
-        scratch_shapes=[blocks] * 7 + [
-            pltpu.VMEM((8, 8, rows, cols), own.dtype),
-            pltpu.VMEM((8, 2, rows, cols), own.dtype),
-            dma((8,)), dma((8,)), dma((8, 8)), dma((64,)), dma((8,)), dma((8,)), dma((8, 2)), dma((8,)),
+        scratch_shapes=[[blocks] * 2] * 7 + [
+            pltpu.VMEM((8, 2, 8, rows, cols), own.dtype),
+            dma((8, 2)), dma((8, 2)), dma((8, 2, 8)), dma((64, 2)), dma((8, 2)),
         ],
         compiler_params=pltpu.CompilerParams(
-            collective_id=collective_id, has_side_effects=True, vmem_limit_bytes=VMEM_LIMIT),
-        cost_estimate=pl.CostEstimate(flops=0, bytes_accessed=40 * moved, transcendentals=0),
-        name="exchange_back" if by_target else "exchange_out",
+            collective_id=0, has_side_effects=True, vmem_limit_bytes=VMEM_LIMIT),
+        cost_estimate=pl.CostEstimate(flops=0, bytes_accessed=250_000_000, transcendentals=0),
+        name="exchange_out",
     )(code, own)
+
+
+def back_kernel(code_ref, own, grad, tokens, weight, out, token_grad, wout,
+                zp0, zp1, zm0, zm1, st_up, st_dn, zp2, zm2, z4, sbuf,
+                gathered, share, crecv, s_own, s_up, s_dn, s_far, y_a, y_b, y_up, y_dn,
+                w_up1, w_up, w_dn1, w_dn,
+                zs, zr, ysend, yrecv, ls, xs, xr, cs, cr, ws, wr, us, ur):
+    p = Place()
+    up, down = p.dev(0, 1), p.dev(0, -1)
+    yup, ydn = p.dev(1), p.dev(-1)
+    far = [p.dev(dx=1), p.dev(dx=-1), p.dev(dx=2)]
+    greet([up, down] + plane_partners(p) + far)
+    first, last = pl.ds(8, 4), pl.ds(8, 4)
+    ups, downs = [], []
+    for hh in range(2):
+        ups.append([remote(own.at[:, hh], zp0[hh], zs.at[0, hh], zr.at[0, hh], up),
+                    remote(zp0[hh], zp1[hh], zs.at[1, hh], zr.at[1, hh], up),
+                    remote(st_up.at[hh], zp2.at[hh], zs.at[2, hh], zr.at[2, hh], up),
+                    remote(zp2.at[hh, first], z4.at[hh, pl.ds(0, 4)], zs.at[3, hh], zr.at[3, hh], up)])
+        downs.append([remote(own.at[:, hh], zm0[hh], zs.at[4, hh], zr.at[4, hh], down),
+                      remote(zm0[hh], zm1[hh], zs.at[5, hh], zr.at[5, hh], down),
+                      remote(st_dn.at[hh], zm2.at[hh], zs.at[6, hh], zr.at[6, hh], down),
+                      remote(zm2.at[hh, last], z4.at[hh, pl.ds(4, 4)], zs.at[7, hh], zr.at[7, hh], down)])
+    sets = [None, zp0, zm0, zp1, zm1]
+    started = []
+
+    def pick(origin, target):
+        return (code_ref[origin * 64 + target] // 8) % 16
+
+    def process(k, hh):
+        origin = p.dp(0, Z_OFF[k], 0)
+        for i, (dy, dc) in enumerate(J_OFF):
+            r = pick(origin, p.dp(dy, 0, dc))
+            sbuf[k, hh, i] = own[r, hh] if k == 0 else sets[k][hh][r]
+        started.append(plane_send(p, out, k, hh, lambda i: sbuf.at[k, hh, i], ysend, yrecv, ls))
+
+    def forward(k, hh, buf):
+        started.append(plane_send(p, out, k, hh, lambda i: buf.at[hh, i], ysend, yrecv, ls))
+
+    def stage(hh, held, staged, way, part):
+        origin = p.dp(0, -2 * way, 0)
+        for i, (dy, dc) in enumerate(J_OFF):
+            staged[hh, i] = held[hh][pick(origin, p.dp(dy, way, dc))]
+        for i in range(4):
+            dy, dc = J_OFF[part + i]
+            staged[hh, 8 + i] = held[hh][pick(origin, p.dp(dy, 2 * way, dc))]
+
+    gathers = [remote(grad, gathered.at[p.x], xs.at[i], xr.at[i], d) for i, d in enumerate(far)]
+    for cp in gathers:
+        cp.start()
+    for hh in range(2):
+        ups[hh][0].start()
+        downs[hh][0].start()
+    gathered[p.x] = grad[...]
+    for hh in range(2):
+        process(0, hh)
+
+    def hop1(hh):
+        ups[hh][0].wait_recv()
+        ups[hh][1].start()
+        downs[hh][0].wait_recv()
+        downs[hh][1].start()
+        process(1, hh)
+        process(2, hh)
+
+    hop1(0)
+    for cp in gathers:
+        cp.wait_recv()
+
+    tn = (((0,), (0,)), ((), ()))
+    nt = (((1,), (1,)), ((), ()))
+    pairs = []
+    for n, dy in enumerate((2, 1, -1, 0)):
+        yy = (p.y + dy + NY) % NY
+
+        @pl.loop(0, 2)
+        def _(r, yy=yy, n=n):
+            cols = pl.ds(pl.multiple_of(r * 256, 256), 256)
+            part = lax.dot_general(gathered[yy, :, cols], tokens[...], tn, preferred_element_type=jnp.float32)
+            share[n, pl.ds(r * 4, 4)] = part.reshape(4, 2, 32, part.shape[1])
+
+        cp = remote(share.at[n, :, 1 - p.c], crecv.at[n], cs.at[n], cr.at[n], p.dev(0, 0, 1))
+        cp.start()
+        pairs.append(cp)
+
+    hop1(1)
+
+    sums = [s_far, s_up, s_dn, s_own]
+    for n in range(4):
+        pairs[n].wait_recv()
+
+        @pl.loop(0, NZ)
+        def _(i, n=n):
+            sums[n][i] = share[n, i, p.c] + crecv[n, i]
+
+        if n == 0:
+            far_up = remote(s_far.at[pl.ds(0, 4)], y_a, ws.at[0], wr.at[0], yup)
+            far_dn = remote(s_far.at[pl.ds(4, 4)], y_b, ws.at[1], wr.at[1], ydn)
+            far_up.start()
+            far_dn.start()
+
+    @pl.loop(0, 4)
+    def _(i):
+        rows = pl.ds(pl.multiple_of(i * 128, 128), 128)
+        total = jnp.zeros((128, weight.shape[0]), jnp.float32)
+        for a in range(4):
+            total += lax.dot_general(gathered[a, rows, :], weight[:, a * 512:(a + 1) * 512], nt,
+                                     preferred_element_type=jnp.float32)
+        token_grad[rows, :] = total.astype(token_grad.dtype)
+
+    far_up.wait_recv()
+
+    @pl.loop(0, 4)
+    def _(i):
+        s_up[i] += y_a[i]
+
+    near_up = remote(s_up, y_up, ws.at[2], wr.at[2], yup)
+    near_up.start()
+    far_dn.wait_recv()
+
+    @pl.loop(0, 4)
+    def _(i):
+        s_dn[4 + i] += y_b[i]
+
+    near_dn = remote(s_dn, y_dn, ws.at[3], wr.at[3], ydn)
+    near_dn.start()
+
+    def hop2(hh):
+        ups[hh][1].wait_recv()
+        stage(hh, zp1, st_up, 1, 0)
+        ups[hh][2].start()
+        downs[hh][1].wait_recv()
+        stage(hh, zm1, st_dn, -1, 4)
+        downs[hh][2].start()
+        process(3, hh)
+        process(4, hh)
+
+    def hop3(hh):
+        ups[hh][2].wait_recv()
+        ups[hh][3].start()
+        downs[hh][2].wait_recv()
+        downs[hh][3].start()
+        forward(5, hh, zp2)
+        forward(6, hh, zm2)
+
+    def hop4(hh):
+        ups[hh][3].wait_recv()
+        downs[hh][3].wait_recv()
+        forward(7, hh, z4)
+
+    hop2(0)
+    hop2(1)
+    near_up.wait_recv()
+    near_dn.wait_recv()
+
+    @pl.loop(0, NZ)
+    def _(i):
+        s_own[i] += y_up[i] + y_dn[i]
+
+    def at(dz):
+        return (p.z + dz + NZ) % NZ
+
+    chain_up = [remote(s_own.at[at(4), pl.ds(0, 16)], w_up1, us.at[0], ur.at[0], up)]
+    chain_dn = [remote(s_own.at[at(4), pl.ds(16, 16)], w_dn1, us.at[4], ur.at[4], down)]
+    for i, dz in enumerate((3, 2, 1)):
+        chain_up.append(remote(s_own.at[at(dz)], w_up.at[i], us.at[1 + i], ur.at[1 + i], up))
+        chain_dn.append(remote(s_own.at[at(-dz)], w_dn.at[i], us.at[5 + i], ur.at[5 + i], down))
+
+    def ring(step):
+        if step == 1:
+            chain_up[0].wait_recv()
+            s_own[at(3), pl.ds(0, 16)] += w_up1[...]
+            chain_dn[0].wait_recv()
+            s_own[at(-3), pl.ds(16, 16)] += w_dn1[...]
+        elif step > 1:
+            chain_up[step - 1].wait_recv()
+            s_own[at(4 - step)] += w_up[step - 2]
+            chain_dn[step - 1].wait_recv()
+            s_own[at(step - 4)] += w_dn[step - 2]
+        if step < 4:
+            chain_up[step].start()
+            chain_dn[step].start()
+
+    ring(0)
+    hop3(0)
+    ring(1)
+    hop3(1)
+    ring(2)
+    hop4(0)
+    ring(3)
+    hop4(1)
+    chain_up[3].wait_recv()
+    chain_dn[3].wait_recv()
+    wout[...] = s_own[p.z] + w_up[2] + w_dn[2]
+
+    for local, sends in started:
+        local.wait()
+        for cp in sends:
+            cp.wait()
+    for hh in range(2):
+        for cp in ups[hh] + downs[hh]:
+            cp.wait_send()
+    for cp in gathers + pairs + [far_up, far_dn, near_up, near_dn] + chain_up + chain_dn:
+        cp.wait_send()
+
+
+def exchange_back(code, own, grad, tokens, weight):
+    n, _, rows, cols = own.shape
+    toks, feats = tokens.shape
+    low, full = jnp.bfloat16, jnp.float32
+    blocks = lambda count: pltpu.VMEM((2, count, rows, cols), low)
+    lump = lambda *lead: pltpu.VMEM(lead + (32, feats), full)
+    dma = pltpu.SemaphoreType.DMA
+    vmem = pl.BlockSpec(memory_space=pltpu.VMEM)
+    return pl.pallas_call(
+        back_kernel,
+        out_shape=[
+            jax.ShapeDtypeStruct((64, 2, rows, cols), low),
+            jax.ShapeDtypeStruct((toks, feats), low),
+            jax.ShapeDtypeStruct((32, feats), full),
+        ],
+        in_specs=[pl.BlockSpec(memory_space=pltpu.SMEM), vmem, vmem, vmem, vmem],
+        out_specs=[pl.BlockSpec(memory_space=pl.ANY), vmem, vmem],
+        scratch_shapes=[[pltpu.VMEM((n, rows, cols), low)] * 2] * 4 + [blocks(12)] * 4 + [
+            blocks(8),
+            pltpu.VMEM((5, 2, 8, rows, cols), low),
+            pltpu.VMEM((4, toks, grad.shape[1]), low),
+            lump(4, NZ, 2), lump(4, NZ), lump(NZ), lump(NZ), lump(NZ), lump(NZ),
+            lump(4), lump(4), lump(NZ), lump(NZ),
+            pltpu.VMEM((16, feats), full), lump(3), pltpu.VMEM((16, feats), full), lump(3),
+            dma((8, 2)), dma((8, 2)), dma((8, 2, 8)), dma((64, 2)), dma((8, 2)),
+            dma((3,)), dma((3,)), dma((4,)), dma((4,)), dma((4,)), dma((4,)), dma((8,)), dma((8,)),
+        ],
+        compiler_params=pltpu.CompilerParams(
+            collective_id=1, has_side_effects=True, vmem_limit_bytes=VMEM_LIMIT),
+        cost_estimate=pl.CostEstimate(flops=0, bytes_accessed=250_000_000, transcendentals=0),
+        name="exchange_back",
+    )(code, own, grad, tokens, weight)
 
 
 def attention_kernel(pos_ref, q_ref, g_ref, kv0_ref, kv1_ref, att_ref, qg_ref, bg_ref):
@@ -265,25 +504,12 @@
     pos = jnp.sum(
         jnp.where(mine[:, None] == slots[None, :], jnp.arange(64, dtype=jnp.int32)[None, :], 0), axis=1)
 
-    store = neighbour_store.transpose(0, 2, 1, 3).reshape(entries_here, heads * near, pair)
-    got = exchange(code, store, False, 0).reshape(64, heads, near, pair)
+    store = neighbour_store.transpose(0, 2, 1, 3).reshape(entries_here, 2, heads * near // 2, pair)
+    got = exchange_out(code, store).reshape(64, heads, near, pair)
     attended, query_grad, block_grad = attention(pos, queries, attended_grad, got)
-
-    full_grad = lax.all_gather(query_grad, "fsdp", axis=1, tiled=True)
-    token_grad = lax.dot_general(
-        full_grad, query_weight, (((1,), (1,)), ((), ())), preferred_element_type=jnp.float32
-    ).astype(jnp.bfloat16)
-    weight_share = lax.psum_scatter(
-        lax.dot_general(
-            full_grad, tokens, (((0,), (0,)), ((), ())), preferred_element_type=jnp.float32
-        ),
-        "dp",
-        scatter_dimension=0,
-        tiled=True,
-    )
+    halves = block_grad.reshape(-1, 2, heads * near // 2, pair)
+    back, token_grad, weight_share = exchange_back(code, halves, query_grad, tokens, query_weight)
     weight_grad = weight_share.T
-
-    back = exchange(code, block_grad.reshape(-1, heads * near, pair), True, 1)
     column = jnp.take(table, slots, axis=0)
     column = lax.dynamic_index_in_dim(column, me, 1, keepdims=False)
     summed = gather_sum(column, back.reshape(64, heads, near, pair))

time: 388 us -> 285 us (0.73)
  Pallas kernels: 311 us -> 250 us
  waiting for transfers between devices: 30.8 us -> 0.02 us
  matrix products: 17.1 us -> 6.87 us
    pallas_call x2, Pallas kernels: 279 us -> 217 us  [the longest x1 133 us: exchange_back(): pl.pallas_call(back_kernel, out_shape=[jax.ShapeDtypeStruct((64, 2, rows,...]
    all_gather x1 -> x0, waiting for transfers between devices: 30.7 us -> none  [on_device(): full_grad = lax.all_gather(query_grad, 'fsdp', axis=1, tiled=True)]
    dot_general x2 -> x0, matrix products: 10.5 us -> none  [the longest x1 7.2 us: on_device(): lax.dot_general(full_grad, tokens, (((0,), (0,)), ((), ())), preferred_el...]
  transfers between devices with their start and end apart: 3 -> 1, of which waited for: 1 -> 0; matrix products, arithmetic and copies ran while one was open for 3% -> 2% of each run, Pallas kernels for 75% -> 30%
where the time goes in v2:
time: 285 us; the launch traced here: 284 us
  Pallas kernels  250 us (88%)
  between operations  14.2 us (5%)
  local copies, waits for them, and re-layouts  8.45 us (3%)
  matrix products  6.87 us (2%)
  other arithmetic  4.09 us (1%)
    pallas_call x1, Pallas kernels, exchange_back(): pl.pallas_call(back_kernel, out_shape=[jax.ShapeDtypeStruct((64, 2, rows,...  133 us
    pallas_call x1, Pallas kernels, exchange_out(): pl.pallas_call(out_kernel, out_shape=jax.ShapeDtypeStruct((64, 2, rows, c...  84.1 us
    pallas_call x1, Pallas kernels, attention(): pl.pallas_call(attention_kernel, grid_spec=pltpu.PrefetchScalarGridSpec(n...  21.8 us
    pallas_call x1, Pallas kernels, gather_sum(): pl.pallas_call(gather_sum_kernel, grid=(heads,), in_specs=[pl.BlockSpec(m...  10.7 us
    dot_general x1, matrix products, on_device(): lax.dot_general(query_weight, tokens, (((0,), (1,)), ((), ())), preferred...  6.87 us
    unnamed x18, local copies, waits for them, and re-layouts  5.88 us
  transfers between devices with their start and end apart: 1, of which 0 were waited for; matrix products, arithmetic and copies ran while one was open for 2% of the time, Pallas kernels for 30%

profile of v2, /device:TPU:1, one launch (start us, length us, event | category | flops | bytes accessed | tf_op | source)
XLA Modules:
  0.0 283.7 jit_solution(16989992960605243853)
XLA Ops:
  7.2 0.0 reduce-scatter.2.cloned.1.call-start
  7.2 6.9 %fusion.9 = f32[2048,512]{0,1:T(8,128)} fusion(bf16[512,1024]{1,0:T(8,128)(2,1)} %tokens.1, bf16[1024,2048]{1,0:T(8,128)(2,1)} %weight.1), kind=kOutput, calls=%fused_computation.41 | convolution fusion | flops 2147483648 | bytes 9437184 | tf_op jit(solution)/shard_map/dot_general | solution.py:485
  14.1 0.0 copy-start.6
  14.1 0.0 copy-start.4
  14.1 0.0 copy-start.5
  14.1 0.0 copy-start.3
  14.1 0.0 copy-start.1
  14.1 0.0 reduce-scatter.2.cloned.1.call-update
  14.2 0.6 copy-done.6
  14.8 0.0 copy-done.4
  14.8 0.0 copy-done.5
  14.8 0.1 multiply_add_fusion
  14.9 0.1 add.202
  14.9 0.1 add.209
  15.0 0.0 copy-done.3
  15.0 0.2 copy.19
  15.2 0.1 reshape.232
  15.4 0.4 select_reduce_fusion
  15.7 0.7 reshape.233.code_ref
  16.4 0.6 gather_fusion
  17.0 0.0 copy-done.1
  17.0 1.0 copy.21
  18.0 84.1 %exchange_out.1 = bf16[64,2,192,128]{3,2,1,0:T(8,128)(2,1)} custom-call(s32[4096]{0:T(1024)} %reshape.233.code_ref, bf16[8,2,192,128]{3,2,1,0:T(8,128)(2,1)} %bitcast.25), custom_call_target="tpu_custom_call" | custom-call | bytes 250000000 | tf_op jit(solution)/shard_map/exchange_out/pallas_call | solution.py:123
  102.2 0.8 fusion.1.code_ref
  103.0 0.7 select_reduce_fusion.1.pos_ref
  103.7 0.0 reduce-scatter.2.cloned.1.call-done
  103.7 2.1 convert_bitcast_fusion.q_ref
  105.8 21.8 %attention.1 = (bf16[512,512]{1,0:T(8,128)(2,1)}, bf16[512,512]{1,0:T(8,128)(2,1)}, bf16[16,8,48,128]{3,2,1,0:T(8,128)(2,1)}) custom-call(s32[16]{0:T(128)} %select_reduce_fusion.1.pos_ref, bf16[512,512]{1,0:T(8,128)(2,1)} %convert_bitcast_fusion.q_ref, bf16[512,512]{1,0:T(8,128)(2,1)} %g_ref.1, bf16[64,8,48,128]{3,2,1,0:T(8,128)(2,1)} %bitcast.21, ...), custom_call_target="tpu_custom_call" | custom-call | tf_op jit(solution)/shard_map/attention/pallas_call | solution.py:420
  127.6 133.3 %exchange_back.1 = (bf16[64,2,192,128]{3,2,1,0:T(8,128)(2,1)}, bf16[512,1024]{1,0:T(8,128)(2,1)}, f32[32,1024]{1,0:T(8,128)}) custom-call(s32[4096]{0:T(1024)} %reshape.233.code_ref, bf16[16,2,192,128]{3,2,1,0:T(8,128)(2,1)} %bitcast.26, bf16[512,512]{1,0:T(8,128)(2,1)} %get-tuple-element.12.grad, bf16[512,1024]{1,0:T(8,128)(2,1)} %tokens.1, ...), custom_call_target="tpu_custom_call" | custom-call | bytes 250000000 | tf_op jit(solution)/shard_map/exchange_back/pallas_call | solution.py:351
  261.0 0.0 copy-start
  261.0 10.7 %gather_sum.1 = f32[8,8,48,128]{3,2,1,0:T(8,128)} custom-call(s32[64]{0:T(128)} %fusion.1.code_ref, bf16[64,8,48,128]{3,2,1,0:T(8,128)(2,1)} %bitcast.23), custom_call_target="tpu_custom_call" | custom-call | tf_op jit(solution)/shard_map/gather_sum/pallas_call | solution.py:458
  271.7 0.0 copy-start.2
  271.7 3.5 %copy.22 = f32[8,48,8,128]{3,2,1,0:T(8,128)} copy(f32[8,48,8,128]{3,1,0,2:T(8,128)} %bitcast.24) | data formatting | bytes 3145728
  275.2 0.0 copy-done
  275.2 1.0 copy.26
  276.2 0.0 copy-done.2
  276.2 0.7 copy.27
  (8 shorter events, 0.1 us)
Async XLA Ops:
  7.2 96.5 %reduce-scatter.2.cloned.1.call-start = ((), (), s32[]{:S(2)}) async-start(), calls=%async_computation.1 | async-start | bytes 5242880 | tf_op jit(solution)/shard_map/reduce_scatter | solution.py:484
  14.1 0.7 copy-start.6
  14.1 0.7 copy-start.4
  14.1 0.7 copy-start.5
  14.1 0.9 copy-start.3
  14.1 2.9 %copy-start.1 = (bf16[8,48,8,128]{3,2,1,0:T(8,128)(2,1)S(1)}, bf16[8,48,8,128]{3,2,1,0:T(8,128)(2,1)}, u32[]{:S(2)}) copy-start(bf16[8,48,8,128]{3,2,1,0:T(8,128)(2,1)} %param.10) | copy-start | bytes 2359300
  261.0 14.2 %copy-start = (bf16[512,1024]{1,0:T(8,128)(2,1)S(1)}, bf16[512,1024]{1,0:T(8,128)(2,1)}, u32[]{:S(2)}) copy-start(bf16[512,1024]{1,0:T(8,128)(2,1)} %get-tuple-element.37) | copy-start | bytes 3145732
  271.7 4.5 %copy-start.2 = (f32[32,1024]{1,0:T(8,128)S(1)}, f32[32,1024]{1,0:T(8,128)}, u32[]{:S(2)}) copy-start(f32[32,1024]{1,0:T(8,128)} %get-tuple-element.14) | copy-start | bytes 393220
Sparse Core Ops, SparseCore 0:
  14.3 53.2 reduce-scatter.1

commit v3 on v2

--- a/solution.py
+++ b/solution.py
@@ -62,12 +62,18 @@
     return local, sends
 
 
-def out_kernel(code_ref, own, out, zp0, zp1, zp2, zm0, zm1, zm2, z4, sbuf,
-               zs, zr, ysend, yrecv, ls):
+def out_kernel(code_ref, own, tokens, weight, out, queries, zp0, zp1, zp2, zm0, zm1, zm2, z4, sbuf,
+               toks, wgt, part, q_a, q_b, q_up, q_dn,
+               zs, zr, ysend, yrecv, ls, fetch, xs, xr):
     p = Place()
     half = own.shape[0] // 2
+    fetches = [pltpu.make_async_copy(tokens, toks, fetch.at[0]),
+               pltpu.make_async_copy(weight, wgt, fetch.at[1])]
+    for cp in fetches:
+        cp.start()
     up, down = p.dev(0, 1), p.dev(0, -1)
-    greet([up, down] + plane_partners(p))
+    xup, xdn = p.dev(dx=1), p.dev(dx=-1)
+    greet([up, down, xup, xdn] + plane_partners(p))
     zp, zm = [zp0, zp1, zp2], [zm0, zm1, zm2]
     lo, hi = pl.ds(0, half), pl.ds(half, half)
     ups, downs = [], []
@@ -95,6 +101,27 @@
         downs[hh][0].start()
     for hh in range(2):
         process(0, hh)
+
+    for cp in fetches:
+        cp.wait()
+    rows, width = queries.shape
+    top, bottom = pl.ds(0, rows // 2), pl.ds(rows // 2, rows // 2)
+    for n, dx in enumerate((2, 1, -1, 0)):
+        cols = pl.ds(pl.multiple_of((p.x + dx + 4) % 4 * width, width), width)
+
+        @pl.loop(0, 4)
+        def _(r, n=n, cols=cols):
+            some = pl.ds(pl.multiple_of(r * (rows // 4), rows // 4), rows // 4)
+            part[n][some, :] = jnp.dot(toks[some, :], wgt[:, cols], preferred_element_type=jnp.float32)
+
+        if n == 0:
+            far_up = remote(part[0].at[top], q_a, xs.at[0], xr.at[0], xup)
+            far_dn = remote(part[0].at[bottom], q_b, xs.at[1], xr.at[1], xdn)
+            far_up.start()
+            far_dn.start()
+
+    near_up = remote(part[1], q_up, xs.at[2], xr.at[2], xup)
+    near_dn = remote(part[2], q_dn, xs.at[3], xr.at[3], xdn)
     for s in range(3):
         for hh in range(2):
             ups[hh][s].wait_recv()
@@ -103,6 +130,16 @@
             downs[hh][s + 1].start()
             process(1 + 2 * s, hh)
             process(2 + 2 * s, hh)
+        if s == 0:
+            far_up.wait_recv()
+            part[1][top, :] += q_a[...]
+            near_up.start()
+            far_dn.wait_recv()
+            part[2][bottom, :] += q_b[...]
+            near_dn.start()
+    near_up.wait_recv()
+    near_dn.wait_recv()
+    queries[...] = (part[3][...] + q_up[...] + q_dn[...]).astype(queries.dtype)
     for hh in range(2):
         ups[hh][3].wait_recv()
         downs[hh][3].wait_recv()
@@ -114,34 +151,50 @@
     for hh in range(2):
         for cp in ups[hh] + downs[hh]:
             cp.wait_send()
-
-
-def exchange_out(code, own):
+    for cp in (far_up, far_dn, near_up, near_dn):
+        cp.wait_send()
+
+
+def exchange_out(code, own, tokens, weight):
     n, _, rows, cols = own.shape
     blocks = pltpu.VMEM((n, rows, cols), own.dtype)
     dma = pltpu.SemaphoreType.DMA
+    hbm = pl.BlockSpec(memory_space=pl.ANY)
+    count, width = tokens.shape[0], weight.shape[1] // 4
+    total = pltpu.VMEM((count, width), jnp.float32)
+    part = pltpu.VMEM((count // 2, width), jnp.float32)
     return pl.pallas_call(
         out_kernel,
-        out_shape=jax.ShapeDtypeStruct((64, 2, rows, cols), own.dtype),
-        in_specs=[pl.BlockSpec(memory_space=pltpu.SMEM), pl.BlockSpec(memory_space=pltpu.VMEM)],
-        out_specs=pl.BlockSpec(memory_space=pl.ANY),
+        out_shape=[
+            jax.ShapeDtypeStruct((64, 2, rows, cols), own.dtype),
+            jax.ShapeDtypeStruct((count, width), own.dtype),
+        ],
+        in_specs=[pl.BlockSpec(memory_space=pltpu.SMEM), pl.BlockSpec(memory_space=pltpu.VMEM), hbm, hbm],
+        out_specs=[hbm, pl.BlockSpec(memory_space=pltpu.VMEM)],
         scratch_shapes=[[blocks] * 2] * 7 + [
             pltpu.VMEM((8, 2, 8, rows, cols), own.dtype),
+            pltpu.VMEM(tokens.shape, tokens.dtype), pltpu.VMEM(weight.shape, weight.dtype),
+            [total] * 4, part, part, total, total,
             dma((8, 2)), dma((8, 2)), dma((8, 2, 8)), dma((64, 2)), dma((8, 2)),
+            dma((2,)), dma((4,)), dma((4,)),
         ],
         compiler_params=pltpu.CompilerParams(
             collective_id=0, has_side_effects=True, vmem_limit_bytes=VMEM_LIMIT),
         cost_estimate=pl.CostEstimate(flops=0, bytes_accessed=250_000_000, transcendentals=0),
         name="exchange_out",
-    )(code, own)
-
-
-def back_kernel(code_ref, own, grad, tokens, weight, out, token_grad, wout,
+    )(code, own, tokens, weight)
+
+
+def back_kernel(code_ref, own, grad, tokens_far, weight_far, out, token_grad, wout,
                 zp0, zp1, zm0, zm1, st_up, st_dn, zp2, zm2, z4, sbuf,
                 gathered, share, crecv, s_own, s_up, s_dn, s_far, y_a, y_b, y_up, y_dn,
-                w_up1, w_up, w_dn1, w_dn,
-                zs, zr, ysend, yrecv, ls, xs, xr, cs, cr, ws, wr, us, ur):
+                w_up1, w_up, w_dn1, w_dn, tokens, weight,
+                zs, zr, ysend, yrecv, ls, xs, xr, cs, cr, ws, wr, us, ur, fetch):
     p = Place()
+    fetches = [pltpu.make_async_copy(tokens_far, tokens, fetch.at[0]),
+               pltpu.make_async_copy(weight_far, weight, fetch.at[1])]
+    for cp in fetches:
+        cp.start()
     up, down = p.dev(0, 1), p.dev(0, -1)
     yup, ydn = p.dev(1), p.dev(-1)
     far = [p.dev(dx=1), p.dev(dx=-1), p.dev(dx=2)]
@@ -202,6 +255,8 @@
     hop1(0)
     for cp in gathers:
         cp.wait_recv()
+    for cp in fetches:
+        cp.wait()
 
     tn = (((0,), (0,)), ((), ()))
     nt = (((1,), (1,)), ((), ()))
@@ -348,6 +403,7 @@
     lump = lambda *lead: pltpu.VMEM(lead + (32, feats), full)
     dma = pltpu.SemaphoreType.DMA
     vmem = pl.BlockSpec(memory_space=pltpu.VMEM)
+    hbm = pl.BlockSpec(memory_space=pl.ANY)
     return pl.pallas_call(
         back_kernel,
         out_shape=[
@@ -355,7 +411,7 @@
             jax.ShapeDtypeStruct((toks, feats), low),
             jax.ShapeDtypeStruct((32, feats), full),
         ],
-        in_specs=[pl.BlockSpec(memory_space=pltpu.SMEM), vmem, vmem, vmem, vmem],
+        in_specs=[pl.BlockSpec(memory_space=pltpu.SMEM), vmem, vmem, hbm, hbm],
         out_specs=[pl.BlockSpec(memory_space=pl.ANY), vmem, vmem],
         scratch_shapes=[[pltpu.VMEM((n, rows, cols), low)] * 2] * 4 + [blocks(12)] * 4 + [
             blocks(8),
@@ -364,8 +420,9 @@
             lump(4, NZ, 2), lump(4, NZ), lump(NZ), lump(NZ), lump(NZ), lump(NZ),
             lump(4), lump(4), lump(NZ), lump(NZ),
             pltpu.VMEM((16, feats), full), lump(3), pltpu.VMEM((16, feats), full), lump(3),
+            pltpu.VMEM(tokens.shape, low), pltpu.VMEM(weight.shape, low),
             dma((8, 2)), dma((8, 2)), dma((8, 2, 8)), dma((64, 2)), dma((8, 2)),
-            dma((3,)), dma((3,)), dma((4,)), dma((4,)), dma((4,)), dma((4,)), dma((8,)), dma((8,)),
+            dma((3,)), dma((3,)), dma((4,)), dma((4,)), dma((4,)), dma((4,)), dma((8,)), dma((8,)), dma((2,)),
         ],
         compiler_params=pltpu.CompilerParams(
             collective_id=1, has_side_effects=True, vmem_limit_bytes=VMEM_LIMIT),
@@ -375,40 +432,53 @@
 
 
 def attention_kernel(pos_ref, q_ref, g_ref, kv0_ref, kv1_ref, att_ref, qg_ref, bg_ref):
-    heads = kv0_ref.shape[1]
-    width = q_ref.shape[1] // heads
-    near = kv0_ref.shape[2]
+    heads, near, pair = kv0_ref.shape[1:]
+    width = pair // 2
     root = 1.0 / math.sqrt(width)
-    zero = jnp.zeros((SPAN, width), jnp.bfloat16)
-    nt = (((1,), (1,)), ((), ()))
-    nn = (((1,), (0,)), ((), ()))
-    tn = (((0,), (0,)), ((), ()))
+    lane = lax.broadcasted_iota(jnp.int32, (SPAN, pair), 1)
+    left = lane < width
+    zero = jnp.zeros((SPAN, pair), jnp.bfloat16)
 
     def dot(a, b, dims):
-        return lax.dot_general(a, b, dims, preferred_element_type=jnp.float32)
-
-    for h in range(heads):
-        cols = slice(h * width, (h + 1) * width)
+        return lax.dot_general(a, b, (dims, ((), ())), preferred_element_type=jnp.float32)
+
+    def swap(a):
+        return jnp.concatenate([a[:, width:], a[:, :width]], axis=1)
+
+    def row(a, b):
+        return jnp.concatenate([a, b], axis=1)
+
+    for h in range(0, heads, 2):
+        cols = slice(h * width, (h + 2) * width)
         q, g = q_ref[:, cols], g_ref[:, cols]
-        kv = jnp.concatenate([kv0_ref[0, h], kv1_ref[0, h]], axis=0)
-        both = jnp.concatenate(
-            [jnp.concatenate([q, zero], axis=1), jnp.concatenate([zero, g], axis=1)], axis=0)
-        raw = dot(both, kv, nt)
-        score = raw[:SPAN] * root
-        prob_grad = raw[SPAN:]
-        weights = jnp.exp(score - jnp.max(score, axis=-1, keepdims=True))
-        probs = weights / jnp.sum(weights, axis=-1, keepdims=True)
+        kv = row(jnp.concatenate([kv0_ref[0, h], kv1_ref[0, h]], axis=0),
+                 jnp.concatenate([kv0_ref[0, h + 1], kv1_ref[0, h + 1]], axis=0))
+        both = jnp.concatenate([
+            row(jnp.where(left, q, zero), zero),
+            row(zero, jnp.where(left, swap(q), zero)),
+            row(jnp.where(left, zero, swap(g)), zero),
+            row(zero, jnp.where(left, zero, g)),
+        ], axis=0)
+        raw = dot(kv, both, ((1,), (1,)))
+        score = raw[:, :pair] * root
+        prob_grad = raw[:, pair:]
+        weights = jnp.exp(score - jnp.max(score, axis=0, keepdims=True))
+        probs = weights / jnp.sum(weights, axis=0, keepdims=True)
         low = probs.astype(jnp.bfloat16)
-        term = jnp.sum(probs * prob_grad, axis=-1, keepdims=True)
+        term = jnp.sum(probs * prob_grad, axis=0, keepdims=True)
         sg = (probs * (prob_grad - term)).astype(jnp.bfloat16)
-        applied = dot(jnp.concatenate([low, sg], axis=0), kv, nn)
-        att_ref[:, cols] = applied[:SPAN, width:].astype(jnp.bfloat16)
-        qg_ref[:, cols] = (applied[SPAN:, :width] * root).astype(jnp.bfloat16)
-        back = dot(jnp.concatenate([sg, low], axis=0), both, tn)
-        lane = lax.broadcasted_iota(jnp.int32, back.shape, 1)
-        back = (back * jnp.where(lane < width, root, 1.0)).astype(jnp.bfloat16)
-        bg_ref[0, h] = back[:near]
-        bg_ref[1, h] = back[near:]
+        applied = dot(row(low, sg), kv, ((0,), (0,)))
+        at_a, at_b = applied[:SPAN, :pair], applied[SPAN:2 * SPAN, pair:]
+        qg_a, qg_b = applied[2 * SPAN:3 * SPAN, :pair], applied[3 * SPAN:, pair:]
+        att_ref[:, cols] = jnp.where(left, swap(at_a), at_b).astype(jnp.bfloat16)
+        qg_ref[:, cols] = (jnp.where(left, qg_a, swap(qg_b)) * root).astype(jnp.bfloat16)
+        back = dot(row(sg, low), both, ((1,), (0,)))
+        scale = jnp.where(lax.broadcasted_iota(jnp.int32, back.shape, 1) % pair < width, root, 1.0)
+        back = (back * scale).astype(jnp.bfloat16)
+        for i in range(2):
+            part = back[:, i * pair:(i + 1) * pair]
+            bg_ref[0, h + i] = part[:near]
+            bg_ref[1, h + i] = part[near:]
 
 
 def attention(pos, queries, grads, blocks):
@@ -436,7 +506,6 @@
 
 
 def gather_sum_kernel(code_ref, blk_ref, out_ref, acc):
-    h = pl.program_id(0)
     acc[...] = jnp.zeros_like(acc)
 
     def body(i, carry):
@@ -445,26 +514,24 @@
         @pl.when(code >= 128)
         def _():
             e = code % 8
-            acc[e] += blk_ref[i, 0].astype(jnp.float32)
+            for h in range(blk_ref.shape[1]):
+                acc[e, h] += blk_ref[i, h].astype(jnp.float32)
 
         return carry
 
     lax.fori_loop(0, 64, body, 0)
-    out_ref[0] = acc[...]
+    for e in range(8):
+        out_ref[e] = jnp.swapaxes(acc[e], 0, 1)
 
 
 def gather_sum(codes, blocks):
     _, heads, near, pair = blocks.shape
     return pl.pallas_call(
         gather_sum_kernel,
-        grid=(heads,),
-        in_specs=[
-            pl.BlockSpec(memory_space=pltpu.SMEM),
-            pl.BlockSpec((64, 1, near, pair), lambda h: (0, h, 0, 0)),
-        ],
-        out_specs=pl.BlockSpec((1, 8, near, pair), lambda h: (h, 0, 0, 0)),
-        out_shape=jax.ShapeDtypeStruct((heads, 8, near, pair), jnp.float32),
-        scratch_shapes=[pltpu.VMEM((8, near, pair), jnp.float32)],
+        in_specs=[pl.BlockSpec(memory_space=pltpu.SMEM), pl.BlockSpec(memory_space=pltpu.VMEM)],
+        out_specs=pl.BlockSpec(memory_space=pltpu.VMEM),
+        out_shape=jax.ShapeDtypeStruct((8, near, heads, pair), jnp.float32),
+        scratch_shapes=[pltpu.VMEM((8, heads, near, pair), jnp.float32)],
         compiler_params=pltpu.CompilerParams(vmem_limit_bytes=VMEM_LIMIT),
         name="gather_sum",
     )(codes, blocks)
@@ -481,16 +548,6 @@
 def on_device(tokens, query_weight, neighbour_store, neighbours, attended_grad):
     entries_here, near, heads, pair = neighbour_store.shape
     me = lax.axis_index("dp")
-    fields = lax.psum_scatter(
-        lax.dot_general(
-            query_weight, tokens, (((0,), (1,)), ((), ())), preferred_element_type=jnp.float32
-        ),
-        "fsdp",
-        scatter_dimension=0,
-        tiled=True,
-    )
-    queries = fields.T.astype(jnp.bfloat16)
-
     refs = neighbours.reshape(64, -1)
     order = jnp.arange(refs.shape[1], dtype=jnp.int32)[None, :]
     word = 128 + 8 * order + refs % entries_here
@@ -505,15 +562,15 @@
         jnp.where(mine[:, None] == slots[None, :], jnp.arange(64, dtype=jnp.int32)[None, :], 0), axis=1)
 
     store = neighbour_store.transpose(0, 2, 1, 3).reshape(entries_here, 2, heads * near // 2, pair)
-    got = exchange_out(code, store).reshape(64, heads, near, pair)
+    got, queries = exchange_out(code, store, tokens, query_weight)
+    got = got.reshape(64, heads, near, pair)
     attended, query_grad, block_grad = attention(pos, queries, attended_grad, got)
     halves = block_grad.reshape(-1, 2, heads * near // 2, pair)
     back, token_grad, weight_share = exchange_back(code, halves, query_grad, tokens, query_weight)
     weight_grad = weight_share.T
     column = jnp.take(table, slots, axis=0)
     column = lax.dynamic_index_in_dim(column, me, 1, keepdims=False)
-    summed = gather_sum(column, back.reshape(64, heads, near, pair))
-    store_grad = summed.transpose(1, 2, 0, 3)
+    store_grad = gather_sum(column, back.reshape(64, heads, near, pair))
     return (attended, token_grad, weight_grad, store_grad)
 
 

time: 285 us -> 246 us (0.86)
  Pallas kernels: 250 us -> 236 us
  between operations: 14.2 us -> 0.76 us
  matrix products: 6.87 us -> 0 us
    pallas_call x1, Pallas kernels: 21.8 us -> 13.5 us  [attention(): pl.pallas_call(attention_kernel, grid_spec=pltpu.PrefetchScalarGridSpec(n...]
    dot_general x1 -> x0, matrix products: 6.87 us -> none  [on_device(): lax.dot_general(query_weight, tokens, (((0,), (1,)), ((), ())), preferred...]
    pallas_call x2, Pallas kernels: 94.8 us -> 90.8 us  [the longest x1 85.3 us: exchange_out(): pl.pallas_call(out_kernel, out_shape=[jax.ShapeDtypeStruct((64, 2, rows,...]
    unnamed x18 -> x7, local copies, waits for them, and re-layouts: 5.88 us -> 2.46 us
  transfers between devices with their start and end apart: 1 -> 0, of which waited for: 0 -> 0; matrix products, arithmetic and copies ran while one was open for 2% -> 0% of each run, Pallas kernels for 30% -> 0%
where the time goes in v3:
time: 246 us
  Pallas kernels  236 us (96%)
  local copies, waits for them, and re-layouts  6.16 us (3%)
  other arithmetic  3.41 us (1%)
    pallas_call x1, Pallas kernels, exchange_back(): pl.pallas_call(back_kernel, out_shape=[jax.ShapeDtypeStruct((64, 2, rows,...  131 us
    pallas_call x1, Pallas kernels, exchange_out(): pl.pallas_call(out_kernel, out_shape=[jax.ShapeDtypeStruct((64, 2, rows,...  85.3 us
    pallas_call x1, Pallas kernels, attention(): pl.pallas_call(attention_kernel, grid_spec=pltpu.PrefetchScalarGridSpec(n...  13.5 us
    pallas_call x1, Pallas kernels, gather_sum(): pl.pallas_call(gather_sum_kernel, in_specs=[pl.BlockSpec(memory_space=plt...  5.56 us

profile of v3, /device:TPU:1, one launch (start us, length us, event | category | flops | bytes accessed | tf_op | source)
XLA Modules:
  0.0 246.0 jit_solution(10015493312266457364)
XLA Ops:
  0.7 0.7 fusion.5
  1.3 0.7 and_select_fusion
  2.0 0.1 multiply_add_fusion
  2.1 0.1 add.200
  2.2 0.1 add.207
  2.3 0.8 copy.15
  3.1 0.1 reshape.232
  3.3 0.8 select_reduce_fusion.1.pos_ref
  4.1 0.4 select_reduce_fusion
  4.5 0.7 reshape.233.code_ref
  5.2 0.6 gather_fusion
  5.8 0.8 fusion.1.code_ref
  6.5 2.1 copy.16
  8.7 85.3 %exchange_out.1 = (bf16[64,2,192,128]{3,2,1,0:T(8,128)(2,1)}, bf16[512,512]{1,0:T(8,128)(2,1)}) custom-call(s32[4096]{0:T(1024)} %reshape.233.code_ref, bf16[8,2,192,128]{3,2,1,0:T(8,128)(2,1)} %bitcast.19, bf16[512,1024]{1,0:T(8,128)(2,1)} %tokens_far.1, bf16[1024,2048]{1,0:T(8,128)(2,1)} %weight_far.1), custom_call_target="tpu_custom_call" | custom-call | bytes 250000000 | tf_op jit(solution)/shard_map/exchange_out/pallas_call | solution.py:166
  93.9 13.5 %attention.1 = (bf16[512,512]{1,0:T(8,128)(2,1)}, bf16[512,512]{1,0:T(8,128)(2,1)}, bf16[16,8,48,128]{3,2,1,0:T(8,128)(2,1)}) custom-call(s32[16]{0:T(128)} %select_reduce_fusion.1.pos_ref, bf16[512,512]{1,0:T(8,128)(2,1)} %get-tuple-element.12.q_ref, bf16[512,512]{1,0:T(8,128)(2,1)} %g_ref.1, bf16[64,8,48,128]{3,2,1,0:T(8,128)(2,1)} %bitcast.16, ...), custom_call_target="tpu_custom_call" | custom-call | tf_op jit(solution)/shard_map/attention/pallas_call | solution.py:490
  107.4 131.4 %exchange_back.1 = (bf16[64,2,192,128]{3,2,1,0:T(8,128)(2,1)}, bf16[512,1024]{1,0:T(8,128)(2,1)}, f32[32,1024]{1,0:T(8,128)}) custom-call(s32[4096]{0:T(1024)} %reshape.233.code_ref, bf16[16,2,192,128]{3,2,1,0:T(8,128)(2,1)} %bitcast.20, bf16[512,512]{1,0:T(8,128)(2,1)} %get-tuple-element.16.grad, bf16[512,1024]{1,0:T(8,128)(2,1)} %tokens_far.1, ...), custom_call_target="tpu_custom_call" | custom-call | bytes 250000000 | tf_op jit(solution)/shard_map/exchange_back/pallas_call | solution.py:407
  238.8 0.0 copy-start
  238.8 0.0 copy-start.1
  238.8 5.6 %gather_sum.1 = f32[8,48,8,128]{3,2,1,0:T(8,128)} custom-call(s32[64]{0:T(128)} %fusion.1.code_ref, bf16[64,8,48,128]{3,2,1,0:T(8,128)(2,1)} %bitcast.18), custom_call_target="tpu_custom_call" | custom-call | tf_op jit(solution)/shard_map/gather_sum/pallas_call | solution.py:529
  244.4 0.0 copy-done
  244.4 1.0 copy.19
  245.4 0.0 copy-done.1
  245.4 0.7 copy.20
  (6 shorter events, 0.1 us)
Async XLA Ops:
  238.8 5.6 %copy-start = (bf16[512,1024]{1,0:T(8,128)(2,1)S(1)}, bf16[512,1024]{1,0:T(8,128)(2,1)}, u32[]{:S(2)}) copy-start(bf16[512,1024]{1,0:T(8,128)(2,1)} %get-tuple-element.29) | copy-start | bytes 3145732
  238.8 6.5 %copy-start.1 = (f32[32,1024]{1,0:T(8,128)S(1)}, f32[32,1024]{1,0:T(8,128)}, u32[]{:S(2)}) copy-start(f32[32,1024]{1,0:T(8,128)} %get-tuple-element.18) | copy-start | bytes 393220

commit v4 on v3

v4 whole, which is shorter than its diff:
```python
import functools
import math

import jax
import jax.numpy as jnp
from jax import lax
from jax.experimental import pallas as pl
from jax.experimental.pallas import tpu as pltpu
from jax.sharding import PartitionSpec as P

SPAN = 64
NY, NZ = 4, 8
MESH = pl.DeviceIdType.MESH
Z_OFF = (0, -1, 1, -2, 2, -3, 3, 4)
J_OFF = ((0, 0), (0, 1), (-1, 0), (-1, 1), (1, 0), (1, 1), (2, 0), (2, 1))
VMEM_LIMIT = 60 * 1024 * 1024


def dp_of(y, z, c):
    return (y * NZ + z) * 2 + c


class Place:
    def __init__(self):
        me = lax.axis_index("dp")
        self.x = lax.axis_index("fsdp")
        self.y, self.z, self.c = me // (2 * NZ), (me // 2) % NZ, me % 2

    def dp(self, dy, dz, dc):
        return dp_of((self.y + dy + NY) % NY, (self.z + dz + NZ) % NZ, (self.c + dc) % 2)

    def dev(self, dy=0, dz=0, dc=0, dx=0):
        return (self.dp(dy, dz, dc), (self.x + dx + 4) % 4)


def greet(devices):
    barrier = pltpu.get_barrier_semaphore()
    for d in devices:
        pl.semaphore_signal(barrier, inc=1, device_id=d, device_id_type=MESH)
    pl.semaphore_wait(barrier, len(devices))


def remote(src, dst, ssem, rsem, d):
    return pltpu.make_async_remote_copy(
        src_ref=src, dst_ref=dst, send_sem=ssem, recv_sem=rsem, device_id=d, device_id_type=MESH)


def plane_partners(p):
    return [p.dev(dy, 0, dc) for dy, dc in J_OFF[1:]]


SLOTS = ((1, 1), (6, 6), (7, 7), (4, 2), (5, 3), (2, 4), (3, 5))


def plane_send(p, out, k, hh, blocks, ysend, yrecv, ls):
    local = pltpu.make_async_copy(blocks(0), out.at[k, hh], ls.at[k, hh])
    local.start()
    sends = []
    for i, j in SLOTS:
        dy, dc = J_OFF[i]
        cp = remote(blocks(i), out.at[j * 8 + k, hh], ysend.at[k, hh, i], yrecv.at[j * 8 + k, hh],
                    p.dev(dy, 0, dc))
        cp.start()
        sends.append(cp)
    return local, sends


def attend(q, g, kv, root):
    pair = q.shape[1]
    width = pair // 2
    left = lax.broadcasted_iota(jnp.int32, q.shape, 1) < width
    zero = jnp.zeros(q.shape, q.dtype)

    def dot(a, b, dims):
        return lax.dot_general(a, b, (dims, ((), ())), preferred_element_type=jnp.float32)

    def swap(a):
        return jnp.concatenate([a[:, width:], a[:, :width]], axis=1)

    def row(a, b):
        return jnp.concatenate([a, b], axis=1)

    both = jnp.concatenate([
        row(jnp.where(left, q, zero), zero),
        row(zero, jnp.where(left, swap(q), zero)),
        row(jnp.where(left, zero, swap(g)), zero),
        row(zero, jnp.where(left, zero, g)),
    ], axis=0)
    raw = dot(kv, both, ((1,), (1,)))
    score = raw[:, :pair] * root
    prob_grad = raw[:, pair:]
    weights = jnp.exp(score - jnp.max(score, axis=0, keepdims=True))
    probs = weights / jnp.sum(weights, axis=0, keepdims=True)
    low = probs.astype(jnp.bfloat16)
    term = jnp.sum(probs * prob_grad, axis=0, keepdims=True)
    sg = (probs * (prob_grad - term)).astype(jnp.bfloat16)
    applied = dot(row(low, sg), kv, ((0,), (0,)))
    at_a, at_b = applied[:SPAN, :pair], applied[SPAN:2 * SPAN, pair:]
    qg_a, qg_b = applied[2 * SPAN:3 * SPAN, :pair], applied[3 * SPAN:, pair:]
    attended = jnp.where(left, swap(at_a), at_b).astype(jnp.bfloat16)
    query_grad = (jnp.where(left, qg_a, swap(qg_b)) * root).astype(jnp.bfloat16)
    back = dot(row(sg, low), both, ((1,), (0,)))
    scale = jnp.where(lax.broadcasted_iota(jnp.int32, back.shape, 1) % pair < width, root, 1.0)
    return attended, query_grad, (back * scale).astype(jnp.bfloat16)


def whole_kernel(near, code_ref, pos_ref, own, tokens_far, weight_far, grads_far,
                 out, attended, token_grad, wout,
                 fp0, fp1, fp2, fm0, fm1, fm2, f4, sbuf, brought, tokens, weight, grads,
                 q_a, q_b, q_up, q_dn, queries, bg,
                 zp0, zp1, zm0, zm1, zp2, zm2, z4, gathered, share, crecv, s_own,
                 y_a, y_b, y_up, y_dn, w_up1, w_up, w_dn1, w_dn,
                 fetch, fs, fr, fysend, fyrecv, qs, qr,
                 zs, zr, zs4, zr4, ysend, yrecv, ls, xs, xr, cs, cr, ws, wr, us, ur):
    p = Place()
    fetches = [pltpu.make_async_copy(tokens_far, tokens, fetch.at[0]),
               pltpu.make_async_copy(weight_far, weight, fetch.at[1]),
               pltpu.make_async_copy(grads_far, grads, fetch.at[2])]
    for cp in fetches:
        cp.start()
    up, down = p.dev(0, 1), p.dev(0, -1)
    yup, ydn = p.dev(1), p.dev(-1)
    xup, xdn, xfar = p.dev(dx=1), p.dev(dx=-1), p.dev(dx=2)
    greet([up, down, xup, xdn, xfar] + plane_partners(p))

    entries = own.shape[0]
    lo, hi = pl.ds(0, entries // 2), pl.ds(entries // 2, entries // 2)
    fups, fdowns = [], []
    for hh in range(2):
        fups.append([remote(own.at[:, hh], fp0[hh], fs.at[0, hh], fr.at[0, hh], up),
                     remote(fp0[hh], fp1[hh], fs.at[1, hh], fr.at[1, hh], up),
                     remote(fp1[hh], fp2[hh], fs.at[2, hh], fr.at[2, hh], up),
                     remote(fp2[hh].at[lo], f4[hh].at[lo], fs.at[3, hh], fr.at[3, hh], up)])
        fdowns.append([remote(own.at[:, hh], fm0[hh], fs.at[4, hh], fr.at[4, hh], down),
                       remote(fm0[hh], fm1[hh], fs.at[5, hh], fr.at[5, hh], down),
                       remote(fm1[hh], fm2[hh], fs.at[6, hh], fr.at[6, hh], down),
                       remote(fm2[hh].at[hi], f4[hh].at[hi], fs.at[7, hh], fr.at[7, hh], down)])
    fsets = [None, fp0, fm0, fp1, fm1, fp2, fm2, f4]
    fsent = [[], []]

    def bring(k, hh):
        origin = p.dp(0, Z_OFF[k], 0)

        def block(i):
            dy, dc = J_OFF[i]
            e = code_ref[p.dp(dy, 0, dc) * 64 + origin] % 8
            return own[e, hh] if k == 0 else fsets[k][hh][e]

        brought[hh][k] = block(0)
        for i, j in SLOTS:
            dy, dc = J_OFF[i]
            sbuf[k, hh, i] = block(i)
            cp = remote(sbuf.at[k, hh, i], brought[hh].at[j * 8 + k], fysend.at[k, hh, i],
                        fyrecv.at[j * 8 + k, hh], p.dev(dy, 0, dc))
            cp.start()
            fsent[hh].append(cp)

    for hh in range(2):
        fups[hh][0].start()
        fdowns[hh][0].start()
    for hh in range(2):
        bring(0, hh)

    for cp in fetches:
        cp.wait()
    rows, width = queries.shape
    half = rows // 2
    parts = [share.at[n, :, pl.ds(0, width)] for n in range(4)]
    for n, dx in enumerate((2, 1, -1, 0)):
        cols = pl.ds(pl.multiple_of((p.x + dx + 4) % 4 * width, width), width)

        @pl.loop(0, 4)
        def _(r, n=n, cols=cols):
            some = pl.ds(pl.multiple_of(r * (rows // 4), rows // 4), rows // 4)
            share[n, some, :width] = jnp.dot(
                tokens[some, :], weight[:, cols], preferred_element_type=jnp.float32)

        if n == 0:
            qfar_up = remote(share.at[0, pl.ds(0, half), pl.ds(0, width)], q_a, qs.at[0], qr.at[0], xup)
            qfar_dn = remote(share.at[0, pl.ds(half, half), pl.ds(0, width)], q_b, qs.at[1], qr.at[1], xdn)
            qfar_up.start()
            qfar_dn.start()

    qnear_up = remote(parts[1], q_up, qs.at[2], qr.at[2], xup)
    qnear_dn = remote(parts[2], q_dn, qs.at[3], qr.at[3], xdn)
    for s in range(3):
        for hh in range(2):
            fups[hh][s].wait_recv()
            fups[hh][s + 1].start()
            fdowns[hh][s].wait_recv()
            fdowns[hh][s + 1].start()
            bring(1 + 2 * s, hh)
            bring(2 + 2 * s, hh)
        if s == 0:
            qfar_up.wait_recv()
            share[1, :half, :width] += q_a[...]
            qnear_up.start()
            qfar_dn.wait_recv()
            share[2, half:, :width] += q_b[...]
            qnear_dn.start()
    for hh in range(2):
        fups[hh][3].wait_recv()
        fdowns[hh][3].wait_recv()
        bring(7, hh)
    qnear_up.wait_recv()
    qnear_dn.wait_recv()
    queries[...] = (share[3, :, :width] + q_up[...] + q_dn[...]).astype(queries.dtype)
    for cp in (qfar_up, qfar_dn, qnear_up, qnear_dn):
        cp.wait_send()

    pair = own.shape[-1]
    root = 1.0 / math.sqrt(pair // 2)
    heads = own.shape[2] // near
    ups, downs = [], []
    for hh in range(2):
        ups.append([remote(bg[hh], zp0[hh], zs.at[0, hh], zr.at[0, hh], up),
                    remote(zp0[hh], zp1[hh], zs.at[1, hh], zr.at[1, hh], up),
                    remote(sbuf.at[5, hh], zp2.at[hh, pl.ds(0, 8)], zs.at[2, hh], zr.at[2, hh], up),
                    remote(zp2.at[hh, pl.ds(8, 4)], z4.at[hh, pl.ds(0, 4)], zs.at[3, hh], zr.at[3, hh], up),
                    remote(sbuf.at[7, hh, pl.ds(0, 4)], zp2.at[hh, pl.ds(8, 4)], zs4.at[0, hh], zr4.at[0, hh], up)])
        downs.append([remote(bg[hh], zm0[hh], zs.at[4, hh], zr.at[4, hh], down),
                      remote(zm0[hh], zm1[hh], zs.at[5, hh], zr.at[5, hh], down),
                      remote(sbuf.at[6, hh], zm2.at[hh, pl.ds(0, 8)], zs.at[6, hh], zr.at[6, hh], down),
                      remote(zm2.at[hh, pl.ds(8, 4)], z4.at[hh, pl.ds(4, 4)], zs.at[7, hh], zr.at[7, hh], down),
                      remote(sbuf.at[7, hh, pl.ds(4, 4)], zm2.at[hh, pl.ds(8, 4)], zs4.at[1, hh], zr4.at[1, hh], down)])
    sets = [None, zp0, zm0, zp1, zm1]
    started, gathers = [], []

    def pick(origin, target):
        return (code_ref[origin * 64 + target] // 8) % 16

    def process(k, hh):
        origin = p.dp(0, Z_OFF[k], 0)
        for i, (dy, dc) in enumerate(J_OFF):
            r = pick(origin, p.dp(dy, 0, dc))
            sbuf[k, hh, i] = bg[hh][r] if k == 0 else sets[k][hh][r]
        started.append(plane_send(p, out, k, hh, lambda i: sbuf.at[k, hh, i], ysend, yrecv, ls))

    def forward(k, hh, buf):
        started.append(plane_send(p, out, k, hh, lambda i: buf.at[hh, i], ysend, yrecv, ls))

    def stage(hh, held, place, way, part):
        origin = p.dp(0, -2 * way, 0)
        for i, (dy, dc) in enumerate(J_OFF):
            sbuf[place, hh, i] = held[hh][pick(origin, p.dp(dy, way, dc))]
        for i in range(4):
            dy, dc = J_OFF[part + i]
            sbuf[7, hh, part + i] = held[hh][pick(origin, p.dp(dy, 2 * way, dc))]

    for hh in range(2):
        for cp in fsent[hh]:
            cp.wait()

        @pl.loop(0, rows // SPAN // 2)
        def _(step, hh=hh):
            for sub in range(2):
                span = step * 2 + sub
                some = pl.ds(pl.multiple_of(span * SPAN, SPAN), SPAN)
                kv0, kv1 = brought[hh][pos_ref[2 * span]], brought[hh][pos_ref[2 * span + 1]]
                for i in range(0, heads, 2):
                    first = (hh * heads + i) * (pair // 2)
                    cols = slice(first, first + pair)
                    kv = jnp.concatenate([
                        jnp.concatenate([kv0[h * near:(h + 1) * near], kv1[h * near:(h + 1) * near]], axis=0)
                        for h in (i, i + 1)], axis=1)
                    at, qg, back = attend(queries[some, cols], grads[some, cols], kv, root)
                    attended[some, cols] = at
                    gathered[p.x, some, cols] = qg
                    for h in range(2):
                        lanes = slice(h * pair, (h + 1) * pair)
                        place = slice((i + h) * near, (i + h + 1) * near)
                        bg[hh][2 * span, place, :] = back[:near, lanes]
                        bg[hh][2 * span + 1, place, :] = back[near:, lanes]

        ups[hh][0].start()
        downs[hh][0].start()
        mine = gathered.at[p.x, :, pl.ds(hh * half, half)]
        for i, d in enumerate((xup, xdn, xfar)):
            cp = remote(mine, mine, xs.at[i, hh], xr.at[i, hh], d)
            cp.start()
            gathers.append(cp)
        process(0, hh)

    def hop1(hh):
        ups[hh][0].wait_recv()
        ups[hh][1].start()
        downs[hh][0].wait_recv()
        downs[hh][1].start()
        process(1, hh)
        process(2, hh)

    hop1(0)
    for cp in gathers:
        cp.wait_recv()

    tn = (((0,), (0,)), ((), ()))
    nt = (((1,), (1,)), ((), ()))
    chunk = 32 * NZ
    kept = p.c * chunk
    pairs = []
    for n, dy in enumerate((2, 1, -1, 0)):
        yy = (p.y + dy + NY) % NY

        @pl.loop(0, 2)
        def _(r, yy=yy, n=n):
            cols = pl.ds(pl.multiple_of(r * chunk, chunk), chunk)
            part = lax.dot_general(gathered[yy, :, cols], tokens[...], tn, preferred_element_type=jnp.float32)
            part = part.reshape(NZ // 2, 2, 32, part.shape[1])
            for core in range(2):
                share[n, pl.ds(pl.multiple_of(core * chunk + r * (chunk // 2), chunk // 2), chunk // 2)] = (
                    part[:, core].reshape(chunk // 2, part.shape[3]))

        cp = remote(share.at[n, pl.ds(pl.multiple_of(chunk - kept, chunk), chunk)], crecv.at[n],
                    cs.at[n], cr.at[n], p.dev(0, 0, 1))
        cp.start()
        pairs.append(cp)

    hop1(1)

    def held(i, count=32):
        return pl.ds(pl.multiple_of(kept + i * 32, 32), count)

    def lump(i):
        return pl.ds(pl.multiple_of(i * 32, 32), 32)

    for n in range(4):
        pairs[n].wait_recv()

        @pl.loop(0, NZ)
        def _(i, n=n):
            share[n, held(i)] += crecv[n, lump(i)]

        if n == 0:
            far_up = remote(share.at[0, held(0, chunk // 2)], y_a, ws.at[0], wr.at[0], yup)
            far_dn = remote(share.at[0, held(4, chunk // 2)], y_b, ws.at[1], wr.at[1], ydn)
            far_up.start()
            far_dn.start()

    @pl.loop(0, 4)
    def _(i):
        some = pl.ds(pl.multiple_of(i * 128, 128), 128)
        total = jnp.zeros((128, weight.shape[0]), jnp.float32)
        for a in range(4):
            total += lax.dot_general(gathered[a, some, :], weight[:, a * 512:(a + 1) * 512], nt,
                                     preferred_element_type=jnp.float32)
        token_grad[some, :] = total.astype(token_grad.dtype)

    far_up.wait_recv()

    @pl.loop(0, 4)
    def _(i):
        share[1, held(i)] += y_a[lump(i)]

    near_up = remote(share.at[1, held(0, chunk)], y_up, ws.at[2], wr.at[2], yup)
    near_up.start()
    far_dn.wait_recv()

    @pl.loop(0, 4)
    def _(i):
        share[2, held(i + 4)] += y_b[lump(i)]

    near_dn = remote(share.at[2, held(0, chunk)], y_dn, ws.at[3], wr.at[3], ydn)
    near_dn.start()

    def hop2(hh):
        ups[hh][1].wait_recv()
        stage(hh, zp1, 5, 1, 0)
        ups[hh][2].start()
        ups[hh][4].start()
        downs[hh][1].wait_recv()
        stage(hh, zm1, 6, -1, 4)
        downs[hh][2].start()
        downs[hh][4].start()
        process(3, hh)
        process(4, hh)

    def hop3(hh):
        ups[hh][4].wait_recv()
        ups[hh][3].start()
        downs[hh][4].wait_recv()
        downs[hh][3].start()
        ups[hh][2].wait_recv()
        forward(5, hh, zp2)
        downs[hh][2].wait_recv()
        forward(6, hh, zm2)

    def hop4(hh):
        ups[hh][3].wait_recv()
        downs[hh][3].wait_recv()
        forward(7, hh, z4)

    hop2(0)
    hop2(1)
    near_up.wait_recv()
    near_dn.wait_recv()

    @pl.loop(0, NZ)
    def _(i):
        s_own[i] = share[3, held(i)] + y_up[lump(i)] + y_dn[lump(i)]

    def at(dz):
        return (p.z + dz + NZ) % NZ

    chain_up = [remote(s_own.at[at(4), pl.ds(0, 16)], w_up1, us.at[0], ur.at[0], up)]
    chain_dn = [remote(s_own.at[at(4), pl.ds(16, 16)], w_dn1, us.at[4], ur.at[4], down)]
    for i, dz in enumerate((3, 2, 1)):
        chain_up.append(remote(s_own.at[at(dz)], w_up.at[i], us.at[1 + i], ur.at[1 + i], up))
        chain_dn.append(remote(s_own.at[at(-dz)], w_dn.at[i], us.at[5 + i], ur.at[5 + i], down))

    def ring(step):
        if step == 1:
            chain_up[0].wait_recv()
            s_own[at(3), pl.ds(0, 16)] += w_up1[...]
            chain_dn[0].wait_recv()
            s_own[at(-3), pl.ds(16, 16)] += w_dn1[...]
        elif step > 1:
            chain_up[step - 1].wait_recv()
            s_own[at(4 - step)] += w_up[step - 2]
            chain_dn[step - 1].wait_recv()
            s_own[at(step - 4)] += w_dn[step - 2]
        if step < 4:
            chain_up[step].start()
            chain_dn[step].start()

    ring(0)
    hop3(0)
    ring(1)
    hop3(1)
    ring(2)
    hop4(0)
    ring(3)
    hop4(1)
    chain_up[3].wait_recv()
    chain_dn[3].wait_recv()
    wout[...] = s_own[p.z] + w_up[2] + w_dn[2]

    for local, sends in started:
        local.wait()
        for cp in sends:
            cp.wait()
    for hh in range(2):
        for cp in fups[hh] + fdowns[hh] + ups[hh] + downs[hh]:
            cp.wait_send()
    for cp in gathers + pairs + [far_up, far_dn, near_up, near_dn] + chain_up + chain_dn:
        cp.wait_send()


def whole(near, code, pos, own, tokens, weight, grads):
    n, _, rows, cols = own.shape
    toks, feats = tokens.shape
    width = weight.shape[1] // 4
    low, full = jnp.bfloat16, jnp.float32
    refs = 16
    chunk = 32 * NZ
    blocks = lambda count: [pltpu.VMEM((count, rows, cols), low)] * 2
    halves = lambda count: pltpu.VMEM((2, count, rows, cols), low)
    wide = lambda *lead: pltpu.VMEM(lead + (feats,), full)
    flat = lambda count: pltpu.VMEM((count, width), full)
    dma = pltpu.SemaphoreType.DMA
    vmem = pl.BlockSpec(memory_space=pltpu.VMEM)
    smem = pl.BlockSpec(memory_space=pltpu.SMEM)
    hbm = pl.BlockSpec(memory_space=pl.ANY)
    return pl.pallas_call(
        functools.partial(whole_kernel, near),
        out_shape=[
            jax.ShapeDtypeStruct((64, 2, rows, cols), low),
            jax.ShapeDtypeStruct((toks, width), low),
            jax.ShapeDtypeStruct((toks, feats), low),
            jax.ShapeDtypeStruct((32, feats), full),
        ],
        in_specs=[smem, smem, vmem, hbm, hbm, hbm],
        out_specs=[hbm, vmem, vmem, vmem],
        scratch_shapes=[blocks(n)] * 7 + [
            pltpu.VMEM((8, 2, 8, rows, cols), low),
            blocks(64),
            pltpu.VMEM(tokens.shape, low), pltpu.VMEM(weight.shape, low), pltpu.VMEM(grads.shape, low),
            flat(toks // 2), flat(toks // 2), flat(toks), flat(toks),
            pltpu.VMEM((toks, width), low),
            blocks(refs), blocks(refs), blocks(refs), blocks(refs), blocks(refs),
            halves(12), halves(12), halves(8),
            pltpu.VMEM((4, toks, width), low),
            wide(4, 2 * chunk), wide(4, chunk), wide(NZ, 32),
            wide(chunk // 2), wide(chunk // 2), wide(chunk), wide(chunk),
            wide(16), wide(3, 32), wide(16), wide(3, 32),
            dma((3,)), dma((8, 2)), dma((8, 2)), dma((8, 2, 8)), dma((64, 2)), dma((4,)), dma((4,)),
            dma((8, 2)), dma((8, 2)), dma((2, 2)), dma((2, 2)), dma((8, 2, 8)), dma((64, 2)), dma((8, 2)),
            dma((3, 2)), dma((3, 2)), dma((4,)), dma((4,)), dma((4,)), dma((4,)), dma((8,)), dma((8,)),
        ],
        compiler_params=pltpu.CompilerParams(
            collective_id=0, has_side_effects=True, vmem_limit_bytes=VMEM_LIMIT),
        cost_estimate=pl.CostEstimate(flops=0, bytes_accessed=500_000_000, transcendentals=0),
        name="whole",
    )(code, pos, own, tokens, weight, grads)


def gather_sum_kernel(code_ref, blk_ref, out_ref, acc):
    acc[...] = jnp.zeros_like(acc)

    def body(i, carry):
        code = code_ref[i]

        @pl.when(code >= 128)
        def _():
            e = code % 8
            for h in range(blk_ref.shape[1]):
                acc[e, h] += blk_ref[i, h].astype(jnp.float32)

        return carry

    lax.fori_loop(0, 64, body, 0)
    for e in range(8):
        out_ref[e] = jnp.swapaxes(acc[e], 0, 1)


def gather_sum(codes, blocks):
    _, heads, near, pair = blocks.shape
    return pl.pallas_call(
        gather_sum_kernel,
        in_specs=[pl.BlockSpec(memory_space=pltpu.SMEM), pl.BlockSpec(memory_space=pltpu.VMEM)],
        out_specs=pl.BlockSpec(memory_space=pltpu.VMEM),
        out_shape=jax.ShapeDtypeStruct((8, near, heads, pair), jnp.float32),
        scratch_shapes=[pltpu.VMEM((8, heads, near, pair), jnp.float32)],
        compiler_params=pltpu.CompilerParams(vmem_limit_bytes=VMEM_LIMIT),
        name="gather_sum",
    )(codes, blocks)


def slot_devices(me):
    y, z, c = me // (2 * NZ), (me // 2) % NZ, me % 2
    ys = jnp.array([j[0] for j in J_OFF], jnp.int32)[:, None]
    cs = jnp.array([j[1] for j in J_OFF], jnp.int32)[:, None]
    zs = jnp.array(Z_OFF, jnp.int32)[None, :]
    return dp_of((y + ys + NY) % NY, (z + zs + NZ) % NZ, (c + cs) % 2).reshape(-1)


def on_device(tokens, query_weight, neighbour_store, neighbours, attended_grad):
    entries_here, near, heads, pair = neighbour_store.shape
    me = lax.axis_index("dp")
    refs = neighbours.reshape(64, -1)
    order = jnp.arange(refs.shape[1], dtype=jnp.int32)[None, :]
    word = 128 + 8 * order + refs % entries_here
    shard = jnp.arange(64, dtype=jnp.int32)
    table = jnp.max(
        jnp.where((refs // entries_here)[:, :, None] == shard, word[:, :, None], 0), axis=1)
    code = table.reshape(-1)

    slots = slot_devices(me)
    mine = lax.dynamic_index_in_dim(refs, me, 0, keepdims=False) // entries_here
    pos = jnp.sum(
        jnp.where(mine[:, None] == slots[None, :], jnp.arange(64, dtype=jnp.int32)[None, :], 0), axis=1)

    store = neighbour_store.transpose(0, 2, 1, 3).reshape(entries_here, 2, heads * near // 2, pair)
    back, attended, token_grad, weight_share = whole(
        near, code, pos, store, tokens, query_weight, attended_grad)
    weight_grad = weight_share.T
    column = jnp.take(table, slots, axis=0)
    column = lax.dynamic_index_in_dim(column, me, 1, keepdims=False)
    store_grad = gather_sum(column, back.reshape(64, heads, near, pair))
    return (attended, token_grad, weight_grad, store_grad)


def solution(mesh):
    return jax.shard_map(
        on_device,
        mesh=mesh,
        in_specs=(
            P("dp", "fsdp"),
            P("fsdp", None),
            P("dp", None, "fsdp", None),
            P(),
            P("dp", "fsdp"),
        ),
        out_specs=(P("dp", "fsdp"), P("dp", "fsdp"), P("fsdp", "dp"), P("dp", None, "fsdp", None)),
        check_vma=False,
    )
```

time: 246 us -> 233 us (0.947)
  Pallas kernels: 236 us -> 222 us
    pallas_call x3 -> x1, Pallas kernels: 230 us -> 217 us  [whole(): pl.pallas_call(functools.partial(whole_kernel, near), out_shape=[jax.Shap...]
where the time goes in v4:
time: 233 us
  Pallas kernels  222 us (95%)
  local copies, waits for them, and re-layouts  6.96 us (3%)
  other arithmetic  3.23 us (1%)
    pallas_call x1, Pallas kernels, whole(): pl.pallas_call(functools.partial(whole_kernel, near), out_shape=[jax.Shap...  217 us
    pallas_call x1, Pallas kernels, gather_sum(): pl.pallas_call(gather_sum_kernel, in_specs=[pl.BlockSpec(memory_space=plt...  5.44 us

profile of v4, /device:TPU:1, one launch (start us, length us, event | category | flops | bytes accessed | tf_op | source)
XLA Modules:
  0.0 232.9 jit_solution(4470699077585213646)
XLA Ops:
  0.7 0.7 fusion.5
  1.3 0.7 and_select_fusion
  2.0 0.1 multiply_add_fusion
  2.1 0.1 add.204
  2.2 0.1 add.207
  2.3 0.8 copy.15
  3.1 0.1 reshape.226
  3.3 0.7 select_reduce_fusion.1.pos_ref
  4.0 0.4 select_reduce_fusion
  4.4 0.7 reshape.227.code_ref
  5.1 0.6 gather_fusion
  5.7 0.7 fusion.1.code_ref
  6.3 2.1 copy.16
  8.5 216.5 %whole.1 = (bf16[64,2,192,128]{3,2,1,0:T(8,128)(2,1)}, bf16[512,512]{1,0:T(8,128)(2,1)}, bf16[512,1024]{1,0:T(8,128)(2,1)}, f32[32,1024]{1,0:T(8,128)}) custom-call(s32[4096]{0:T(1024)} %reshape.227.code_ref, s32[16]{0:T(128)} %select_reduce_fusion.1.pos_ref, bf16[8,2,192,128]{3,2,1,0:T(8,128)(2,1)} %bitcast.15, bf16[512,1024]{1,0:T(8,128)(2,1)} %tokens_far.1, ...), custom_call_target="tpu_custom_call" | custom-call | bytes 500000000 | tf_op jit(solution)/shard_map/whole/pallas_call | solution.py:463
  225.0 0.0 copy-start.1
  225.0 0.0 copy-start
  225.0 0.0 copy-start.2
  225.0 5.4 %gather_sum.1 = f32[8,48,8,128]{3,2,1,0:T(8,128)} custom-call(s32[64]{0:T(128)} %fusion.1.code_ref, bf16[64,8,48,128]{3,2,1,0:T(8,128)(2,1)} %bitcast.14), custom_call_target="tpu_custom_call" | custom-call | tf_op jit(solution)/shard_map/gather_sum/pallas_call | solution.py:517
  230.5 0.0 copy-done.1
  230.5 0.8 copy.20
  231.3 0.0 copy-done
  231.3 1.0 copy.21
  232.3 0.0 copy-done.2
  232.3 0.7 copy.22
  (6 shorter events, 0.1 us)
Async XLA Ops:
  225.0 5.5 %copy-start.1 = (bf16[512,512]{1,0:T(8,128)(2,1)S(1)}, bf16[512,512]{1,0:T(8,128)(2,1)}, u32[]{:S(2)}) copy-start(bf16[512,512]{1,0:T(8,128)(2,1)} %get-tuple-element.20) | copy-start | bytes 1572868
  225.0 6.3 %copy-start = (bf16[512,1024]{1,0:T(8,128)(2,1)S(1)}, bf16[512,1024]{1,0:T(8,128)(2,1)}, u32[]{:S(2)}) copy-start(bf16[512,1024]{1,0:T(8,128)(2,1)} %get-tuple-element.21) | copy-start | bytes 3145732
  225.0 7.2 %copy-start.2 = (f32[32,1024]{1,0:T(8,128)S(1)}, f32[32,1024]{1,0:T(8,128)}, u32[]{:S(2)}) copy-start(f32[32,1024]{1,0:T(8,128)} %get-tuple-element.10) | copy-start | bytes 393220

commit v5 on v4

--- a/solution.py
+++ b/solution.py
@@ -9,6 +9,7 @@
 from jax.sharding import PartitionSpec as P
 
 SPAN = 64
+PARTS = 4
 NY, NZ = 4, 8
 MESH = pl.DeviceIdType.MESH
 Z_OFF = (0, -1, 1, -2, 2, -3, 3, 4)
@@ -104,7 +105,7 @@
     return attended, query_grad, (back * scale).astype(jnp.bfloat16)
 
 
-def whole_kernel(near, code_ref, pos_ref, own, tokens_far, weight_far, grads_far,
+def whole_kernel(near, code_ref, refs_ref, own, tokens_far, weight_far, grads_far,
                  out, attended, token_grad, wout,
                  fp0, fp1, fp2, fm0, fm1, fm2, f4, sbuf, brought, tokens, weight, grads,
                  q_a, q_b, q_up, q_dn, queries, bg,
@@ -126,7 +127,7 @@
     entries = own.shape[0]
     lo, hi = pl.ds(0, entries // 2), pl.ds(entries // 2, entries // 2)
     fups, fdowns = [], []
-    for hh in range(2):
+    for hh in range(PARTS):
         fups.append([remote(own.at[:, hh], fp0[hh], fs.at[0, hh], fr.at[0, hh], up),
                      remote(fp0[hh], fp1[hh], fs.at[1, hh], fr.at[1, hh], up),
                      remote(fp1[hh], fp2[hh], fs.at[2, hh], fr.at[2, hh], up),
@@ -136,7 +137,7 @@
                        remote(fm1[hh], fm2[hh], fs.at[6, hh], fr.at[6, hh], down),
                        remote(fm2[hh].at[hi], f4[hh].at[hi], fs.at[7, hh], fr.at[7, hh], down)])
     fsets = [None, fp0, fm0, fp1, fm1, fp2, fm2, f4]
-    fsent = [[], []]
+    fsent = [[] for _ in range(PARTS)]
 
     def bring(k, hh):
         origin = p.dp(0, Z_OFF[k], 0)
@@ -155,10 +156,10 @@
             cp.start()
             fsent[hh].append(cp)
 
-    for hh in range(2):
+    for hh in range(PARTS):
         fups[hh][0].start()
         fdowns[hh][0].start()
-    for hh in range(2):
+    for hh in range(PARTS):
         bring(0, hh)
 
     for cp in fetches:
@@ -184,7 +185,7 @@
     qnear_up = remote(parts[1], q_up, qs.at[2], qr.at[2], xup)
     qnear_dn = remote(parts[2], q_dn, qs.at[3], qr.at[3], xdn)
     for s in range(3):
-        for hh in range(2):
+        for hh in range(PARTS):
             fups[hh][s].wait_recv()
             fups[hh][s + 1].start()
             fdowns[hh][s].wait_recv()
@@ -198,7 +199,7 @@
             qfar_dn.wait_recv()
             share[2, half:, :width] += q_b[...]
             qnear_dn.start()
-    for hh in range(2):
+    for hh in range(PARTS):
         fups[hh][3].wait_recv()
         fdowns[hh][3].wait_recv()
         bring(7, hh)
@@ -212,7 +213,7 @@
     root = 1.0 / math.sqrt(pair // 2)
     heads = own.shape[2] // near
     ups, downs = [], []
-    for hh in range(2):
+    for hh in range(PARTS):
         ups.append([remote(bg[hh], zp0[hh], zs.at[0, hh], zr.at[0, hh], up),
                     remote(zp0[hh], zp1[hh], zs.at[1, hh], zr.at[1, hh], up),
                     remote(sbuf.at[5, hh], zp2.at[hh, pl.ds(0, 8)], zs.at[2, hh], zr.at[2, hh], up),
@@ -247,7 +248,14 @@
             dy, dc = J_OFF[part + i]
             sbuf[7, hh, part + i] = held[hh][pick(origin, p.dp(dy, 2 * way, dc))]
 
-    for hh in range(2):
+    def slot_of(r):
+        shard = refs_ref[p.dp(0, 0, 0) * 16 + r] // entries
+        dy = (shard // (2 * NZ) + NY - p.y) % NY
+        dz = ((shard // 2) % NZ + NZ - p.z) % NZ
+        j = jnp.where(dy == 0, 0, jnp.where(dy == 1, 4, jnp.where(dy == 2, 6, 2))) + (shard + p.c) % 2
+        return j * 8 + jnp.where(dz < 4, 2 * dz, 2 * NZ - 1 - 2 * dz)
+
+    def attend_part(hh):
         for cp in fsent[hh]:
             cp.wait()
 
@@ -256,7 +264,7 @@
             for sub in range(2):
                 span = step * 2 + sub
                 some = pl.ds(pl.multiple_of(span * SPAN, SPAN), SPAN)
-                kv0, kv1 = brought[hh][pos_ref[2 * span]], brought[hh][pos_ref[2 * span + 1]]
+                kv0, kv1 = brought[hh][slot_of(2 * span)], brought[hh][slot_of(2 * span + 1)]
                 for i in range(0, heads, 2):
                     first = (hh * heads + i) * (pair // 2)
                     cols = slice(first, first + pair)
@@ -274,7 +282,7 @@
 
         ups[hh][0].start()
         downs[hh][0].start()
-        mine = gathered.at[p.x, :, pl.ds(hh * half, half)]
+        mine = gathered.at[p.x, :, pl.ds(hh * (width // PARTS), width // PARTS)]
         for i, d in enumerate((xup, xdn, xfar)):
             cp = remote(mine, mine, xs.at[i, hh], xr.at[i, hh], d)
             cp.start()
@@ -289,7 +297,10 @@
         process(1, hh)
         process(2, hh)
 
-    hop1(0)
+    for hh in range(PARTS):
+        attend_part(hh)
+    for hh in range(PARTS // 2):
+        hop1(hh)
     for cp in gathers:
         cp.wait_recv()
 
@@ -315,7 +326,8 @@
         cp.start()
         pairs.append(cp)
 
-    hop1(1)
+    for hh in range(PARTS // 2, PARTS):
+        hop1(hh)
 
     def held(i, count=32):
         return pl.ds(pl.multiple_of(kept + i * 32, 32), count)
@@ -365,12 +377,12 @@
     def hop2(hh):
         ups[hh][1].wait_recv()
         stage(hh, zp1, 5, 1, 0)
+        ups[hh][4].start()
         ups[hh][2].start()
-        ups[hh][4].start()
         downs[hh][1].wait_recv()
         stage(hh, zm1, 6, -1, 4)
+        downs[hh][4].start()
         downs[hh][2].start()
-        downs[hh][4].start()
         process(3, hh)
         process(4, hh)
 
@@ -389,8 +401,8 @@
         downs[hh][3].wait_recv()
         forward(7, hh, z4)
 
-    hop2(0)
-    hop2(1)
+    for hh in range(PARTS):
+        hop2(hh)
     near_up.wait_recv()
     near_dn.wait_recv()
 
@@ -422,14 +434,14 @@
             chain_up[step].start()
             chain_dn[step].start()
 
-    ring(0)
-    hop3(0)
-    ring(1)
-    hop3(1)
-    ring(2)
-    hop4(0)
-    ring(3)
-    hop4(1)
+    for hh in range(PARTS):
+        hop3(hh)
+        if hh % (PARTS // 2) == PARTS // 2 - 1:
+            ring(hh // (PARTS // 2))
+    for hh in range(PARTS):
+        hop4(hh)
+        if hh % (PARTS // 2) == PARTS // 2 - 1:
+            ring(2 + hh // (PARTS // 2))
     chain_up[3].wait_recv()
     chain_dn[3].wait_recv()
     wout[...] = s_own[p.z] + w_up[2] + w_dn[2]
@@ -438,22 +450,22 @@
         local.wait()
         for cp in sends:
             cp.wait()
-    for hh in range(2):
+    for hh in range(PARTS):
         for cp in fups[hh] + fdowns[hh] + ups[hh] + downs[hh]:
             cp.wait_send()
     for cp in gathers + pairs + [far_up, far_dn, near_up, near_dn] + chain_up + chain_dn:
         cp.wait_send()
 
 
-def whole(near, code, pos, own, tokens, weight, grads):
+def whole(near, code, refs_flat, own, tokens, weight, grads):
     n, _, rows, cols = own.shape
     toks, feats = tokens.shape
     width = weight.shape[1] // 4
     low, full = jnp.bfloat16, jnp.float32
     refs = 16
     chunk = 32 * NZ
-    blocks = lambda count: [pltpu.VMEM((count, rows, cols), low)] * 2
-    halves = lambda count: pltpu.VMEM((2, count, rows, cols), low)
+    blocks = lambda count: [pltpu.VMEM((count, rows, cols), low)] * PARTS
+    halves = lambda count: pltpu.VMEM((PARTS, count, rows, cols), low)
     wide = lambda *lead: pltpu.VMEM(lead + (feats,), full)
     flat = lambda count: pltpu.VMEM((count, width), full)
     dma = pltpu.SemaphoreType.DMA
@@ -463,7 +475,7 @@
     return pl.pallas_call(
         functools.partial(whole_kernel, near),
         out_shape=[
-            jax.ShapeDtypeStruct((64, 2, rows, cols), low),
+            jax.ShapeDtypeStruct((64, PARTS, rows, cols), low),
             jax.ShapeDtypeStruct((toks, width), low),
             jax.ShapeDtypeStruct((toks, feats), low),
             jax.ShapeDtypeStruct((32, feats), full),
@@ -471,7 +483,7 @@
         in_specs=[smem, smem, vmem, hbm, hbm, hbm],
         out_specs=[hbm, vmem, vmem, vmem],
         scratch_shapes=[blocks(n)] * 7 + [
-            pltpu.VMEM((8, 2, 8, rows, cols), low),
+            pltpu.VMEM((8, PARTS, 8, rows, cols), low),
             blocks(64),
             pltpu.VMEM(tokens.shape, low), pltpu.VMEM(weight.shape, low), pltpu.VMEM(grads.shape, low),
             flat(toks // 2), flat(toks // 2), flat(toks), flat(toks),
@@ -482,42 +494,56 @@
             wide(4, 2 * chunk), wide(4, chunk), wide(NZ, 32),
             wide(chunk // 2), wide(chunk // 2), wide(chunk), wide(chunk),
             wide(16), wide(3, 32), wide(16), wide(3, 32),
-            dma((3,)), dma((8, 2)), dma((8, 2)), dma((8, 2, 8)), dma((64, 2)), dma((4,)), dma((4,)),
-            dma((8, 2)), dma((8, 2)), dma((2, 2)), dma((2, 2)), dma((8, 2, 8)), dma((64, 2)), dma((8, 2)),
-            dma((3, 2)), dma((3, 2)), dma((4,)), dma((4,)), dma((4,)), dma((4,)), dma((8,)), dma((8,)),
+            dma((3,)), dma((8, PARTS)), dma((8, PARTS)), dma((8, PARTS, 8)), dma((64, PARTS)), dma((4,)), dma((4,)),
+            dma((8, PARTS)), dma((8, PARTS)), dma((2, PARTS)), dma((2, PARTS)),
+            dma((8, PARTS, 8)), dma((64, PARTS)), dma((8, PARTS)),
+            dma((3, PARTS)), dma((3, PARTS)), dma((4,)), dma((4,)), dma((4,)), dma((4,)), dma((8,)), dma((8,)),
         ],
         compiler_params=pltpu.CompilerParams(
             collective_id=0, has_side_effects=True, vmem_limit_bytes=VMEM_LIMIT),
         cost_estimate=pl.CostEstimate(flops=0, bytes_accessed=500_000_000, transcendentals=0),
         name="whole",
-    )(code, pos, own, tokens, weight, grads)
+    )(code, refs_flat, own, tokens, weight, grads)
 
 
 def gather_sum_kernel(code_ref, blk_ref, out_ref, acc):
-    acc[...] = jnp.zeros_like(acc)
-
-    def body(i, carry):
-        code = code_ref[i]
-
-        @pl.when(code >= 128)
-        def _():
-            e = code % 8
-            for h in range(blk_ref.shape[1]):
-                acc[e, h] += blk_ref[i, h].astype(jnp.float32)
-
-        return carry
-
-    lax.fori_loop(0, 64, body, 0)
-    for e in range(8):
-        out_ref[e] = jnp.swapaxes(acc[e], 0, 1)
+    p = Place()
+    step = pl.program_id(0)
+
+    @pl.when(step == 0)
+    def _():
+        acc[...] = jnp.zeros_like(acc)
+
+    dy = jnp.where(step == 0, 0, jnp.where(step == 1, -1, jnp.where(step == 2, 1, 2)))
+    column = ((p.y + dy + NY) % NY) * (2 * NZ)
+    me = p.dp(0, 0, 0)
+    for core in range(2):
+        for k in range(8):
+            source = column + ((p.z + Z_OFF[k] + NZ) % NZ) * 2 + (p.c + core) % 2
+            code = code_ref[source * 64 + me]
+
+            @pl.when(code >= 128)
+            def _(code=code, i=core * 8 + k):
+                e = code % 8
+                for h in range(blk_ref.shape[1]):
+                    acc[e, h] += blk_ref[i, h].astype(jnp.float32)
+
+    @pl.when(step == 3)
+    def _():
+        for e in range(8):
+            out_ref[e] = jnp.swapaxes(acc[e], 0, 1)
 
 
 def gather_sum(codes, blocks):
     _, heads, near, pair = blocks.shape
     return pl.pallas_call(
         gather_sum_kernel,
-        in_specs=[pl.BlockSpec(memory_space=pltpu.SMEM), pl.BlockSpec(memory_space=pltpu.VMEM)],
-        out_specs=pl.BlockSpec(memory_space=pltpu.VMEM),
+        grid=(4,),
+        in_specs=[
+            pl.BlockSpec(memory_space=pltpu.SMEM),
+            pl.BlockSpec((16, heads, near, pair), lambda i: (i, 0, 0, 0)),
+        ],
+        out_specs=pl.BlockSpec((8, near, heads, pair), lambda i: (0, 0, 0, 0)),
         out_shape=jax.ShapeDtypeStruct((8, near, heads, pair), jnp.float32),
         scratch_shapes=[pltpu.VMEM((8, heads, near, pair), jnp.float32)],
         compiler_params=pltpu.CompilerParams(vmem_limit_bytes=VMEM_LIMIT),
@@ -525,18 +551,10 @@
     )(codes, blocks)
 
 
-def slot_devices(me):
-    y, z, c = me // (2 * NZ), (me // 2) % NZ, me % 2
-    ys = jnp.array([j[0] for j in J_OFF], jnp.int32)[:, None]
-    cs = jnp.array([j[1] for j in J_OFF], jnp.int32)[:, None]
-    zs = jnp.array(Z_OFF, jnp.int32)[None, :]
-    return dp_of((y + ys + NY) % NY, (z + zs + NZ) % NZ, (c + cs) % 2).reshape(-1)
-
-
 def on_device(tokens, query_weight, neighbour_store, neighbours, attended_grad):
     entries_here, near, heads, pair = neighbour_store.shape
-    me = lax.axis_index("dp")
-    refs = neighbours.reshape(64, -1)
+    flat = neighbours.reshape(-1)
+    refs = flat.reshape(64, -1)
     order = jnp.arange(refs.shape[1], dtype=jnp.int32)[None, :]
     word = 128 + 8 * order + refs % entries_here
     shard = jnp.arange(64, dtype=jnp.int32)
@@ -544,18 +562,11 @@
         jnp.where((refs // entries_here)[:, :, None] == shard, word[:, :, None], 0), axis=1)
     code = table.reshape(-1)
 
-    slots = slot_devices(me)
-    mine = lax.dynamic_index_in_dim(refs, me, 0, keepdims=False) // entries_here
-    pos = jnp.sum(
-        jnp.where(mine[:, None] == slots[None, :], jnp.arange(64, dtype=jnp.int32)[None, :], 0), axis=1)
-
-    store = neighbour_store.transpose(0, 2, 1, 3).reshape(entries_here, 2, heads * near // 2, pair)
+    store = neighbour_store.transpose(0, 2, 1, 3).reshape(entries_here, PARTS, heads * near // PARTS, pair)
     back, attended, token_grad, weight_share = whole(
-        near, code, pos, store, tokens, query_weight, attended_grad)
+        near, code, flat, store, tokens, query_weight, attended_grad)
     weight_grad = weight_share.T
-    column = jnp.take(table, slots, axis=0)
-    column = lax.dynamic_index_in_dim(column, me, 1, keepdims=False)
-    store_grad = gather_sum(column, back.reshape(64, heads, near, pair))
+    store_grad = gather_sum(code, back.reshape(64, heads, near, pair))
     return (attended, token_grad, weight_grad, store_grad)
 
 

time: 233 us -> 225 us (0.966)
  Pallas kernels: 222 us -> 216 us
  other arithmetic: 3.23 us -> 0.4 us
    pallas_call x1, Pallas kernels: 217 us -> 210 us  [whole(): pl.pallas_call(functools.partial(whole_kernel, near), out_shape=[jax.Shap...]
where the time goes in v5:
time: 225 us; the launch traced here: 224 us
  Pallas kernels  216 us (96%)
  local copies, waits for them, and re-layouts  6.96 us (3%)
    pallas_call x1, Pallas kernels, whole(): pl.pallas_call(functools.partial(whole_kernel, near), out_shape=[jax.Shap...  210 us
    pallas_call x1, Pallas kernels, gather_sum(): pl.pallas_call(gather_sum_kernel, grid=(4,), in_specs=[pl.BlockSpec(memor...  5.73 us

profile of v5, /device:TPU:1, one launch (start us, length us, event | category | flops | bytes accessed | tf_op | source)
XLA Modules:
  0.0 224.2 jit_solution(11742537506371784917)
XLA Ops:
  0.6 0.8 copy.13
  1.5 0.8 reshape.90.refs_ref
  2.2 0.1 reshape_reshape.3
  2.4 0.4 select_reduce_fusion
  2.8 0.7 reshape.89.code_ref
  3.5 2.1 copy.15
  5.6 210.4 %whole.1 = (bf16[64,4,96,128]{3,2,1,0:T(8,128)(2,1)}, bf16[512,512]{1,0:T(8,128)(2,1)}, bf16[512,1024]{1,0:T(8,128)(2,1)}, f32[32,1024]{1,0:T(8,128)}) custom-call(s32[4096]{0:T(1024)} %reshape.89.code_ref, s32[1024]{0:T(1024)} %reshape.90.refs_ref, bf16[8,4,96,128]{3,2,1,0:T(8,128)(2,1)} %bitcast.5, bf16[512,1024]{1,0:T(8,128)(2,1)} %tokens_far.1, ...), custom_call_target="tpu_custom_call" | custom-call | bytes 500000000 | tf_op jit(solution)/shard_map/whole/pallas_call | solution.py:475
  216.0 0.0 copy-start.1
  216.0 0.0 copy-start
  216.0 0.0 copy-start.2
  216.1 5.7 %gather_sum.1 = f32[8,48,8,128]{3,2,1,0:T(8,128)} custom-call(s32[4096]{0:T(1024)} %reshape.89.code_ref, bf16[64,8,48,128]{3,2,1,0:T(8,128)(2,1)} %bitcast.4), custom_call_target="tpu_custom_call" | custom-call | tf_op jit(solution)/shard_map/gather_sum/pallas_call | solution.py:539
  221.8 0.0 copy-done.1
  221.8 0.8 copy.19
  222.6 0.0 copy-done
  222.6 1.0 copy.20
  223.6 0.0 copy-done.2
  223.6 0.7 copy.21
  (2 shorter events, 0.0 us)
Async XLA Ops:
  216.0 5.8 %copy-start.1 = (bf16[512,512]{1,0:T(8,128)(2,1)S(1)}, bf16[512,512]{1,0:T(8,128)(2,1)}, u32[]{:S(2)}) copy-start(bf16[512,512]{1,0:T(8,128)(2,1)} %get-tuple-element.18) | copy-start | bytes 1572868
  216.0 6.5 %copy-start = (bf16[512,1024]{1,0:T(8,128)(2,1)S(1)}, bf16[512,1024]{1,0:T(8,128)(2,1)}, u32[]{:S(2)}) copy-start(bf16[512,1024]{1,0:T(8,128)(2,1)} %get-tuple-element.19) | copy-start | bytes 3145732
  216.0 7.5 %copy-start.2 = (f32[32,1024]{1,0:T(8,128)S(1)}, f32[32,1024]{1,0:T(8,128)}, u32[]{:S(2)}) copy-start(f32[32,1024]{1,0:T(8,128)} %get-tuple-element.10) | copy-start | bytes 393220

commit v6 on v5

--- a/solution.py
+++ b/solution.py
@@ -46,6 +46,10 @@
         src_ref=src, dst_ref=dst, send_sem=ssem, recv_sem=rsem, device_id=d, device_id_type=MESH)
 
 
+def drain(ref, sem):
+    pltpu.make_async_copy(ref, ref, sem).wait()
+
+
 def plane_partners(p):
     return [p.dev(dy, 0, dc) for dy, dc in J_OFF[1:]]
 
@@ -54,16 +58,10 @@
 
 
 def plane_send(p, out, k, hh, blocks, ysend, yrecv, ls):
-    local = pltpu.make_async_copy(blocks(0), out.at[k, hh], ls.at[k, hh])
-    local.start()
-    sends = []
+    pltpu.make_async_copy(blocks(0), out.at[k, hh], ls).start()
     for i, j in SLOTS:
         dy, dc = J_OFF[i]
-        cp = remote(blocks(i), out.at[j * 8 + k, hh], ysend.at[k, hh, i], yrecv.at[j * 8 + k, hh],
-                    p.dev(dy, 0, dc))
-        cp.start()
-        sends.append(cp)
-    return local, sends
+        remote(blocks(i), out.at[j * 8 + k, hh], ysend, yrecv, p.dev(dy, 0, dc)).start()
 
 
 def attend(q, g, kv, root):
@@ -137,7 +135,6 @@
                        remote(fm1[hh], fm2[hh], fs.at[6, hh], fr.at[6, hh], down),
                        remote(fm2[hh].at[hi], f4[hh].at[hi], fs.at[7, hh], fr.at[7, hh], down)])
     fsets = [None, fp0, fm0, fp1, fm1, fp2, fm2, f4]
-    fsent = [[] for _ in range(PARTS)]
 
     def bring(k, hh):
         origin = p.dp(0, Z_OFF[k], 0)
@@ -151,10 +148,8 @@
         for i, j in SLOTS:
             dy, dc = J_OFF[i]
             sbuf[k, hh, i] = block(i)
-            cp = remote(sbuf.at[k, hh, i], brought[hh].at[j * 8 + k], fysend.at[k, hh, i],
-                        fyrecv.at[j * 8 + k, hh], p.dev(dy, 0, dc))
-            cp.start()
-            fsent[hh].append(cp)
+            remote(sbuf.at[k, hh, i], brought[hh].at[j * 8 + k], fysend.at[hh],
+                   fyrecv.at[hh], p.dev(dy, 0, dc)).start()
 
     for hh in range(PARTS):
         fups[hh][0].start()
@@ -225,7 +220,7 @@
                       remote(zm2.at[hh, pl.ds(8, 4)], z4.at[hh, pl.ds(4, 4)], zs.at[7, hh], zr.at[7, hh], down),
                       remote(sbuf.at[7, hh, pl.ds(4, 4)], zm2.at[hh, pl.ds(8, 4)], zs4.at[1, hh], zr4.at[1, hh], down)])
     sets = [None, zp0, zm0, zp1, zm1]
-    started, gathers = [], []
+    gathers = []
 
     def pick(origin, target):
         return (code_ref[origin * 64 + target] // 8) % 16
@@ -235,10 +230,10 @@
         for i, (dy, dc) in enumerate(J_OFF):
             r = pick(origin, p.dp(dy, 0, dc))
             sbuf[k, hh, i] = bg[hh][r] if k == 0 else sets[k][hh][r]
-        started.append(plane_send(p, out, k, hh, lambda i: sbuf.at[k, hh, i], ysend, yrecv, ls))
+        plane_send(p, out, k, hh, lambda i: sbuf.at[k, hh, i], ysend, yrecv, ls)
 
     def forward(k, hh, buf):
-        started.append(plane_send(p, out, k, hh, lambda i: buf.at[hh, i], ysend, yrecv, ls))
+        plane_send(p, out, k, hh, lambda i: buf.at[hh, i], ysend, yrecv, ls)
 
     def stage(hh, held, place, way, part):
         origin = p.dp(0, -2 * way, 0)
@@ -256,8 +251,8 @@
         return j * 8 + jnp.where(dz < 4, 2 * dz, 2 * NZ - 1 - 2 * dz)
 
     def attend_part(hh):
-        for cp in fsent[hh]:
-            cp.wait()
+        drain(brought[hh].at[pl.ds(8, 56)], fyrecv.at[hh])
+        drain(brought[hh].at[pl.ds(8, 56)], fysend.at[hh])
 
         @pl.loop(0, rows // SPAN // 2)
         def _(step, hh=hh):
@@ -446,10 +441,9 @@
     chain_dn[3].wait_recv()
     wout[...] = s_own[p.z] + w_up[2] + w_dn[2]
 
-    for local, sends in started:
-        local.wait()
-        for cp in sends:
-            cp.wait()
+    drain(out.at[pl.ds(0, 8)], ls)
+    drain(out.at[pl.ds(8, 56)], ysend)
+    drain(out.at[pl.ds(8, 56)], yrecv)
     for hh in range(PARTS):
         for cp in fups[hh] + fdowns[hh] + ups[hh] + downs[hh]:
             cp.wait_send()
@@ -494,9 +488,9 @@
             wide(4, 2 * chunk), wide(4, chunk), wide(NZ, 32),
             wide(chunk // 2), wide(chunk // 2), wide(chunk), wide(chunk),
             wide(16), wide(3, 32), wide(16), wide(3, 32),
-            dma((3,)), dma((8, PARTS)), dma((8, PARTS)), dma((8, PARTS, 8)), dma((64, PARTS)), dma((4,)), dma((4,)),
+            dma((3,)), dma((8, PARTS)), dma((8, PARTS)), dma((PARTS,)), dma((PARTS,)), dma((4,)), dma((4,)),
             dma((8, PARTS)), dma((8, PARTS)), dma((2, PARTS)), dma((2, PARTS)),
-            dma((8, PARTS, 8)), dma((64, PARTS)), dma((8, PARTS)),
+            dma, dma, dma,
             dma((3, PARTS)), dma((3, PARTS)), dma((4,)), dma((4,)), dma((4,)), dma((4,)), dma((8,)), dma((8,)),
         ],
         compiler_params=pltpu.CompilerParams(

time: 225 us -> 215 us (0.956)
  Pallas kernels: 216 us -> 207 us
    pallas_call x1, Pallas kernels: 210 us -> 201 us  [whole(): pl.pallas_call(functools.partial(whole_kernel, near), out_shape=[jax.Shap...]
where the time goes in v6:
time: 215 us
  Pallas kernels  207 us (96%)
  local copies, waits for them, and re-layouts  6.96 us (3%)
    pallas_call x1, Pallas kernels, whole(): pl.pallas_call(functools.partial(whole_kernel, near), out_shape=[jax.Shap...  201 us
    pallas_call x1, Pallas kernels, gather_sum(): pl.pallas_call(gather_sum_kernel, grid=(4,), in_specs=[pl.BlockSpec(memor...  6.12 us

profile of v6, /device:TPU:1, one launch (start us, length us, event | category | flops | bytes accessed | tf_op | source)
XLA Modules:
  0.0 215.2 jit_solution(7469466822069152489)
XLA Ops:
  0.6 0.8 copy.13
  1.5 0.8 reshape.90.refs_ref
  2.2 0.1 reshape_reshape.3
  2.4 0.4 select_reduce_fusion
  2.8 0.7 reshape.89.code_ref
  3.5 2.1 copy.15
  5.6 201.1 %whole.1 = (bf16[64,4,96,128]{3,2,1,0:T(8,128)(2,1)}, bf16[512,512]{1,0:T(8,128)(2,1)}, bf16[512,1024]{1,0:T(8,128)(2,1)}, f32[32,1024]{1,0:T(8,128)}) custom-call(s32[4096]{0:T(1024)} %reshape.89.code_ref, s32[1024]{0:T(1024)} %reshape.90.refs_ref, bf16[8,4,96,128]{3,2,1,0:T(8,128)(2,1)} %bitcast.5, bf16[512,1024]{1,0:T(8,128)(2,1)} %tokens_far.1, ...), custom_call_target="tpu_custom_call" | custom-call | bytes 500000000 | tf_op jit(solution)/shard_map/whole/pallas_call | solution.py:469
  206.7 0.0 copy-start.1
  206.7 0.0 copy-start
  206.7 0.0 copy-start.2
  206.7 6.1 %gather_sum.1 = f32[8,48,8,128]{3,2,1,0:T(8,128)} custom-call(s32[4096]{0:T(1024)} %reshape.89.code_ref, bf16[64,8,48,128]{3,2,1,0:T(8,128)(2,1)} %bitcast.4), custom_call_target="tpu_custom_call" | custom-call | tf_op jit(solution)/shard_map/gather_sum/pallas_call | solution.py:533
  212.8 0.0 copy-done.1
  212.8 0.8 copy.19
  213.6 0.0 copy-done
  213.6 1.0 copy.20
  214.6 0.0 copy-done.2
  214.6 0.7 copy.21
  (2 shorter events, 0.0 us)
Async XLA Ops:
  206.7 6.2 %copy-start.1 = (bf16[512,512]{1,0:T(8,128)(2,1)S(1)}, bf16[512,512]{1,0:T(8,128)(2,1)}, u32[]{:S(2)}) copy-start(bf16[512,512]{1,0:T(8,128)(2,1)} %get-tuple-element.18) | copy-start | bytes 1572868
  206.7 6.9 %copy-start = (bf16[512,1024]{1,0:T(8,128)(2,1)S(1)}, bf16[512,1024]{1,0:T(8,128)(2,1)}, u32[]{:S(2)}) copy-start(bf16[512,1024]{1,0:T(8,128)(2,1)} %get-tuple-element.19) | copy-start | bytes 3145732
  206.7 7.9 %copy-start.2 = (f32[32,1024]{1,0:T(8,128)S(1)}, f32[32,1024]{1,0:T(8,128)}, u32[]{:S(2)}) copy-start(f32[32,1024]{1,0:T(8,128)} %get-tuple-element.10) | copy-start | bytes 393220
